TPU v7x, 256 devices: a whole 4x4x8 slice. The times are simulated.
256 devices in a mesh: seq: 64 (over y, z, x_hi), mp: 4 (over x_lo, core).
Axes of the slice: x: 4 (x_hi: 2, x_lo: 2; x = x_hi * 2 + x_lo), y: 4, z: 8, core: 2. Of those that a mesh axis runs over, the one named last changes fastest.
Arguments:
- queries: bfloat16 [32768, 2048], P('seq', 'mp'), may hold values from -5 to 5
- key_rows: bfloat16 [32768, 2048], P('seq', 'mp'), may hold values from -5 to 5
- value_rows: bfloat16 [32768, 2048], P('seq', 'mp'), may hold values from -6 to 6
- out_weight: bfloat16 [2048, 2048], P('mp'), may hold values from -3 to 3
- grad_out: bfloat16 [32768, 2048], P('seq', 'mp'), may hold values from -1.5 to 1.5
- offsets: int32 [2, 16], P(None, 'mp'), may hold values from 0 to 63, as said below
Outputs:
- mixed: bfloat16 [32768, 2048], P('seq', 'mp')
- query_grad: bfloat16 [32768, 2048], P('seq', 'mp')
- key_grad: bfloat16 [32768, 2048], P('seq', 'mp')
- value_grad: bfloat16 [32768, 2048], P('seq', 'mp')
Inputs may be any that keep to these rules, and one draw needn't show every extreme that they name: offsets[0, h] lies in 0 to 3 and offsets[1, h] in 0 to 63; in each row some head has the largest value and another head has 0.
All inputs are finite; a program needn't handle non-finite values.
Results may differ from a plain program's by a relative error of at most 0.024.
Values may be sent and summed in bfloat16 or wider, within the bound.
A program may use at most 128 MiB of HBM per device.

v0:
```python
import jax
import jax.numpy as jnp
from jax import lax
from jax.sharding import PartitionSpec as P

HEAD_DIM = 128
GROUP = 4


def passed_along(array, axis, by):
    size = lax.axis_size(axis)
    pairs = [(i, i + by) for i in range(size) if 0 <= i + by < size]
    return lax.ppermute(array, axis, pairs)


def pick_rows(stacked, stride, offsets):
    shaped = stacked.reshape(
        (stacked.shape[0], stacked.shape[1] // stride, stride) + stacked.shape[2:]
    )
    parts = [
        lax.dynamic_index_in_dim(shaped[head_index], offsets[head_index], 1, keepdims=False)
        for head_index in range(stacked.shape[0])
    ]
    return jnp.stack(parts)


def place_rows(values, stride, offsets, filler):
    chosen = jnp.arange(stride, dtype=jnp.int32)[None, :] == offsets[:, None]
    chosen = chosen.reshape((chosen.shape[0], 1, stride) + (1,) * (values.ndim - 2))
    spread = jnp.where(chosen, values[:, :, None], filler)
    return spread.reshape((values.shape[0], values.shape[1] * stride) + values.shape[2:])


def split_heads(matrix):
    return matrix.reshape(matrix.shape[0], -1, HEAD_DIM).transpose(1, 0, 2)


def merge_heads(stacked):
    return stacked.transpose(1, 0, 2).reshape(stacked.shape[1], -1)


def masked_scores(query_seg, key_seg, visible, score_scale):
    scores = (
        jnp.einsum("hid,hjd->hij", query_seg, key_seg, preferred_element_type=jnp.float32)
        * score_scale
    )
    return jnp.where(visible[None], scores, -jnp.inf)


def mix_values(exp_scores, value_seg):
    return jnp.einsum(
        "hij,hjd->hid",
        exp_scores.astype(jnp.bfloat16),
        value_seg,
        preferred_element_type=jnp.float32,
    )


def level_backward(exp_scores, totals_seg, inner_seg, key_seg, value_seg, grad_seg, score_scale):
    probability = exp_scores / totals_seg[..., None]
    prob_low = probability.astype(jnp.bfloat16)
    prob_grad = jnp.einsum("hid,hjd->hij", grad_seg, value_seg, preferred_element_type=jnp.float32)
    score_grad = (probability * (prob_grad - inner_seg[..., None])).astype(jnp.bfloat16)
    query_term = score_scale * jnp.einsum(
        "hij,hjd->hid", score_grad, key_seg, preferred_element_type=jnp.float32
    )
    return (prob_low, score_grad, query_term)


def key_value_terms(prob_low, score_grad, query_seg, grad_seg, score_scale):
    key_term = score_scale * jnp.einsum(
        "hij,hid->hjd", score_grad, query_seg, preferred_element_type=jnp.float32
    )
    value_term = jnp.einsum("hij,hid->hjd", prob_low, grad_seg, preferred_element_type=jnp.float32)
    return (key_term, value_term)


def local(queries, key_rows, value_rows, out_weight, grad_out, offsets):
    tok_rows = queries.shape[0]
    seq_count = lax.axis_size("seq")
    seq_index = lax.axis_index("seq")
    group_pos = seq_index % GROUP
    score_scale = HEAD_DIM ** (-0.5)
    near_rows = tok_rows // GROUP
    far_count = tok_rows // seq_count
    out_grad = lax.dot_general(
        lax.all_gather(grad_out, "mp", axis=1, tiled=True),
        out_weight,
        (((1,), (1,)), ((), ())),
        preferred_element_type=jnp.float32,
    ).astype(jnp.bfloat16)
    query_all = split_heads(queries)
    key_all = split_heads(key_rows)
    value_all = split_heads(value_rows)
    grad_all = split_heads(out_grad)
    head_count = query_all.shape[0]
    near_offsets = offsets[0]
    far_offsets = offsets[1]
    near_query = pick_rows(query_all, GROUP, near_offsets)
    near_key_own = pick_rows(key_all, GROUP, near_offsets)
    near_value_own = pick_rows(value_all, GROUP, near_offsets)
    far_query = pick_rows(query_all, seq_count, far_offsets)
    far_key_own = pick_rows(key_all, seq_count, far_offsets)
    far_value_own = pick_rows(value_all, seq_count, far_offsets)
    key_blocks = [near_key_own]
    value_blocks = [near_value_own]
    for block_index in range(1, GROUP):
        got_key, got_value = passed_along((near_key_own, near_value_own), "seq", block_index)
        key_blocks.append(got_key)
        value_blocks.append(got_value)
    held_keys = jnp.stack(key_blocks)
    held_values = jnp.stack(value_blocks)
    near_keys = held_keys.transpose(1, 0, 2, 3).reshape(head_count, GROUP * near_rows, HEAD_DIM)
    near_values = held_values.transpose(1, 0, 2, 3).reshape(head_count, GROUP * near_rows, HEAD_DIM)
    far_keys, far_values = (
        lax.all_gather(far_key_own, "seq", axis=1, tiled=True),
        lax.all_gather(far_value_own, "seq", axis=1, tiled=True),
    )
    own_rows = jnp.arange(tok_rows)
    causal = own_rows[:, None] >= own_rows[None, :]
    near_cols = jnp.arange(GROUP * near_rows)
    near_block = near_cols // near_rows
    near_visible = (near_block[None, :] <= group_pos) & (
        (near_block[None, :] > 0)
        | (near_cols[None, :] % near_rows <= jnp.arange(near_rows)[:, None])
    )
    far_cols = jnp.arange(seq_count * far_count)
    far_source = far_cols // far_count
    far_visible = (far_source[None, :] < seq_index) | (far_source[None, :] == seq_index) & (
        far_cols[None, :] % far_count <= jnp.arange(far_count)[:, None]
    )
    local_scores = masked_scores(query_all, key_all, causal, score_scale)
    near_scores = masked_scores(near_query, near_keys, near_visible, score_scale)
    far_scores = masked_scores(far_query, far_keys, far_visible, score_scale)
    row_max = jnp.max(local_scores, -1)
    row_max = jnp.maximum(
        row_max, place_rows(jnp.max(near_scores, -1), GROUP, near_offsets, -jnp.inf)
    )
    row_max = jnp.maximum(
        row_max, place_rows(jnp.max(far_scores, -1), seq_count, far_offsets, -jnp.inf)
    )
    local_exp = jnp.exp(local_scores - row_max[..., None])
    near_max = pick_rows(row_max, GROUP, near_offsets)
    far_max = pick_rows(row_max, seq_count, far_offsets)
    near_exp = jnp.exp(near_scores - near_max[..., None])
    far_exp = jnp.exp(far_scores - far_max[..., None])
    totals = (
        jnp.sum(local_exp, -1)
        + place_rows(jnp.sum(near_exp, -1), GROUP, near_offsets, 0.0)
        + place_rows(jnp.sum(far_exp, -1), seq_count, far_offsets, 0.0)
    )
    weighted = (
        mix_values(local_exp, value_all)
        + place_rows(mix_values(near_exp, near_values), GROUP, near_offsets, 0.0)
        + place_rows(mix_values(far_exp, far_values), seq_count, far_offsets, 0.0)
    )
    attended = (weighted / totals[..., None]).astype(jnp.bfloat16)
    attended_flat = merge_heads(attended)
    partial_out = jnp.dot(attended_flat, out_weight, preferred_element_type=jnp.float32)
    mixed = lax.psum_scatter(partial_out, "mp", scatter_dimension=1, tiled=True).astype(
        jnp.bfloat16
    )
    row_inner = jnp.sum(grad_all.astype(jnp.float32) * attended.astype(jnp.float32), -1)
    near_grad = pick_rows(grad_all, GROUP, near_offsets)
    far_grad = pick_rows(grad_all, seq_count, far_offsets)
    near_totals = pick_rows(totals, GROUP, near_offsets)
    near_inner = pick_rows(row_inner, GROUP, near_offsets)
    far_totals = pick_rows(totals, seq_count, far_offsets)
    far_inner = pick_rows(row_inner, seq_count, far_offsets)
    local_prob, local_sgrad, local_qterm = level_backward(
        local_exp, totals, row_inner, key_all, value_all, grad_all, score_scale
    )
    local_kterm, local_vterm = key_value_terms(
        local_prob, local_sgrad, query_all, grad_all, score_scale
    )
    near_prob, near_sgrad, near_qterm = level_backward(
        near_exp, near_totals, near_inner, near_keys, near_values, near_grad, score_scale
    )
    far_prob, far_sgrad, far_qterm = level_backward(
        far_exp, far_totals, far_inner, far_keys, far_values, far_grad, score_scale
    )
    near_kterm, near_vterm = key_value_terms(
        near_prob, near_sgrad, near_query, near_grad, score_scale
    )
    key_parts = near_kterm.reshape(head_count, GROUP, near_rows, HEAD_DIM).transpose(1, 0, 2, 3)
    value_parts = near_vterm.reshape(head_count, GROUP, near_rows, HEAD_DIM).transpose(1, 0, 2, 3)
    near_key_grad = key_parts[0]
    near_value_grad = value_parts[0]
    for block_index in range(1, GROUP):
        got_key, got_value = passed_along(
            (key_parts[block_index], value_parts[block_index]), "seq", -block_index
        )
        near_key_grad = near_key_grad + got_key
        near_value_grad = near_value_grad + got_value
    key_term = score_scale * jnp.einsum(
        "hij,hid->jhd", far_sgrad, far_query, preferred_element_type=jnp.float32
    )
    value_term = jnp.einsum("hij,hid->jhd", far_prob, far_grad, preferred_element_type=jnp.float32)
    far_sums = lax.psum_scatter(
        jnp.concatenate(
            [
                key_term.reshape(far_count * lax.axis_size("seq"), -1),
                value_term.reshape(far_count * lax.axis_size("seq"), -1),
            ],
            1,
        ),
        "seq",
        scatter_dimension=0,
        tiled=True,
    )
    far_sums = far_sums.reshape(far_count, 2, head_count, HEAD_DIM)
    far_key_grad = far_sums[:, 0].transpose(1, 0, 2)
    far_value_grad = far_sums[:, 1].transpose(1, 0, 2)
    query_grad = (
        local_qterm
        + place_rows(near_qterm, GROUP, near_offsets, 0.0)
        + place_rows(far_qterm, seq_count, far_offsets, 0.0)
    )
    key_grad = (
        local_kterm
        + place_rows(near_key_grad, GROUP, near_offsets, 0.0)
        + place_rows(far_key_grad, seq_count, far_offsets, 0.0)
    )
    value_grad = (
        local_vterm
        + place_rows(near_value_grad, GROUP, near_offsets, 0.0)
        + place_rows(far_value_grad, seq_count, far_offsets, 0.0)
    )
    return (
        mixed,
        merge_heads(query_grad.astype(jnp.bfloat16)),
        merge_heads(key_grad.astype(jnp.bfloat16)),
        merge_heads(value_grad.astype(jnp.bfloat16)),
    )


def solution(mesh):
    return jax.shard_map(
        local,
        mesh=mesh,
        in_specs=(
            P("seq", "mp"),
            P("seq", "mp"),
            P("seq", "mp"),
            P("mp", None),
            P("seq", "mp"),
            P(None, "mp"),
        ),
        out_specs=(P("seq", "mp"), P("seq", "mp"), P("seq", "mp"), P("seq", "mp")),
        check_vma=False,
    )
```

profile of v0, /device:TPU:1, one launch (start us, length us, event | category | flops | bytes accessed | tf_op | source)
XLA Modules:
  0.0 965.1 jit_solution(12602437794968632917)
XLA Ops:
  37.3 6.1 collective-permute-start
  43.5 3.6 collective-permute-start.1
  47.0 4.9 collective-permute-start.2
  62.0 2.0 copy.414
  64.0 1.9 fusion.104
  80.2 162.6 %all_gather.9 = bf16[4,512,128]{2,1,0:T(8,128)(2,1)} all-gather(bf16[4,8,128]{2,1,0:T(8,128)(2,1)S(1)} %pad_maximum_fusion.10), channel_id=1, replica_groups=mesh['seq'=64,'mp'=4] {'seq'}, dimensions={1}, use_global_device_ids=true | all-gather | bytes 532480 | tf_op jit(solution)/shard_map/all_gather | solution.py:116
  242.8 159.5 %all_gather.10 = bf16[4,512,128]{2,1,0:T(8,128)(2,1)} all-gather(bf16[4,8,128]{2,1,0:T(8,128)(2,1)S(1)} %pad_maximum_fusion.11), channel_id=1, replica_groups=mesh['seq'=64,'mp'=4] {'seq'}, dimensions={1}, use_global_device_ids=true | all-gather | bytes 532480 | tf_op jit(solution)/shard_map/all_gather | solution.py:117
  402.3 3.4 fusion
  411.6 2.9 convolution_convert_fusion
  429.5 5.1 collective-permute-start.3
  434.6 1.9 collective-permute-start.4
  436.5 1.9 collective-permute-start.5
  457.2 3.1 fusion.2
  466.8 2.5 copy.426
  477.6 2.6 copy.421
  480.2 5.3 multiply_reduce_fusion
  488.9 2.7 pad_maximum_fusion
  491.7 3.0 copy.474
  494.7 4.3 fusion.108
  507.5 3.4 fusion.6
  517.6 4.2 multiply_convert_fusion
  525.9 2.5 copy.435
  530.7 2.5 copy.440
  534.5 2.8 fusion.26
  537.4 2.1 copy.459
  541.2 4.6 collective-permute-done.8
  548.6 315.1 %reduce-scatter.7.cloned.1.call-done = f32[8,1024]{1,0:T(8,128)} async-done(((f32[512,1024]{1,0:T(8,128)}), f32[8,1024]{1,0:T(8,128)}) %reduce-scatter.7.cloned.1.call-update) | async-done | bytes 32784
  866.2 1.9 add_convert_fusion
  870.4 2.7 copy.450
  873.0 3.0 fusion.25
  877.1 79.4 %reduce-scatter.5.cloned.1.call-done = f32[512,512]{1,0:T(8,128)} async-done(((f32[512,2048]{1,0:T(8,128)}), f32[512,512]{1,0:T(8,128)}) %reduce-scatter.5.cloned.1.call-update) | async-done | bytes 1048592 | tf_op jit(solution)/shard_map/reduce_scatter | solution.py:160
  956.5 2.1 convert_element_type.55
  (352 shorter events, 129.2 us)
Async XLA Ops:
  7.2 404.5 %copy-start = (bf16[512,2048]{1,0:T(8,128)(2,1)S(1)}, bf16[512,2048]{1,0:T(8,128)(2,1)}, u32[]{:S(2)}) copy-start(bf16[512,2048]{1,0:T(8,128)(2,1)} %param.9) | copy-start | bytes 6291460
  7.2 404.4 %all-gather.2.cloned.1.call-start = ((), (), s32[]{:S(2)}) async-start(), calls=%async_computation.3 | async-start | bytes 2621440 | tf_op jit(solution)/shard_map/all_gather | solution.py:87
  18.5 59.6 %copy-start.35 = (s32[2,4]{1,0:T(2,128)S(1)}, s32[2,4]{1,0:T(2,128)}, u32[]{:S(2)}) copy-start(s32[2,4]{1,0:T(2,128)} %param.11) | copy-start | bytes 100
  35.1 29.0 %copy-start.14 = (bf16[1,512,128]{2,1,0:T(8,128)(2,1)}, bf16[1,512,128]{2,1,0:T(8,128)(2,1)S(1)}, u32[]{:S(2)}) copy-start(bf16[1,512,128]{2,1,0:T(8,128)(2,1)S(1)} %copy.397) | copy-start | bytes 393220
  37.3 368.4 %collective-permute-start = (bf16[4,128,128]{2,1,0:T(8,128)(2,1)}, bf16[4,128,128]{2,1,0:T(8,128)(2,1)}, u32[]{:S(2)}, u32[]{:S(2)}) collective-permute-start(bf16[4,128,128]{2,1,0:T(8,128)(2,1)} %get-tuple-element.72), channel_id=1, source_target_pairs={{0,4},{4,8},{8,12},{12,16},{16,20},{20,24},{24,28},{28,32},{32,36}... | collective-permute-start | bytes 393224 | tf_op jit(solution)/shard_map/ppermute | solution.py:13
  43.5 362.3 %collective-permute-start.1 = (bf16[4,128,128]{2,1,0:T(8,128)(2,1)}, bf16[4,128,128]{2,1,0:T(8,128)(2,1)}, u32[]{:S(2)}, u32[]{:S(2)}) collective-permute-start(bf16[4,128,128]{2,1,0:T(8,128)(2,1)} %get-tuple-element.72), channel_id=1, source_target_pairs={{0,8},{4,12},{8,16},{12,20},{16,24},{20,28},{24,32},{28,36},{32,40... | collective-permute-start | bytes 393224 | tf_op jit(solution)/shard_map/ppermute | solution.py:13
  47.0 358.8 %collective-permute-start.2 = (bf16[4,128,128]{2,1,0:T(8,128)(2,1)}, bf16[4,128,128]{2,1,0:T(8,128)(2,1)}, u32[]{:S(2)}, u32[]{:S(2)}) collective-permute-start(bf16[4,128,128]{2,1,0:T(8,128)(2,1)} %get-tuple-element.72), channel_id=1, source_target_pairs={{0,12},{4,16},{8,20},{12,24},{16,28},{20,32},{24,36},{28,40},{32,4... | collective-permute-start | bytes 393224 | tf_op jit(solution)/shard_map/ppermute | solution.py:13
  51.9 811.8 %reduce-scatter.7.cloned.1.call-start = ((), (), s32[]{:S(2)}) async-start(), calls=%async_computation.4 | async-start | bytes 2129920
  242.8 165.0 %copy-start.21 = (bf16[128,1,128]{2,0,1:T(8,128)(2,1)S(1)}, bf16[128,1,128]{2,0,1:T(8,128)(2,1)}, u32[]{:S(2)}) copy-start(bf16[128,1,128]{2,0,1:T(8,128)(2,1)} %copy.560) | copy-start | bytes 98308
  242.8 165.0 %copy-start.23 = (bf16[128,1,128]{2,0,1:T(8,128)(2,1)S(1)}, bf16[128,1,128]{2,0,1:T(8,128)(2,1)}, u32[]{:S(2)}) copy-start(bf16[128,1,128]{2,0,1:T(8,128)(2,1)} %copy.561) | copy-start | bytes 98308
  242.8 165.0 %copy-start.24 = (bf16[128,1,128]{2,0,1:T(8,128)(2,1)S(1)}, bf16[128,1,128]{2,0,1:T(8,128)(2,1)}, u32[]{:S(2)}) copy-start(bf16[128,1,128]{2,0,1:T(8,128)(2,1)} %copy.562) | copy-start | bytes 98308
  242.8 165.0 %copy-start.25 = (bf16[128,1,128]{2,0,1:T(8,128)(2,1)S(1)}, bf16[128,1,128]{2,0,1:T(8,128)(2,1)}, u32[]{:S(2)}) copy-start(bf16[128,1,128]{2,0,1:T(8,128)(2,1)} %copy.563) | copy-start | bytes 98308
  429.5 43.4 %collective-permute-start.3 = (bf16[4,128,128]{2,1,0:T(8,128)(2,1)}, bf16[4,128,128]{2,1,0:T(8,128)(2,1)}, u32[]{:S(2)}, u32[]{:S(2)}) collective-permute-start(bf16[4,128,128]{2,1,0:T(8,128)(2,1)} %get-tuple-element.70), channel_id=1, source_target_pairs={{0,4},{4,8},{8,12},{12,16},{16,20},{20,24},{24,28},{28,32},{32,36}... | collective-permute-start | bytes 393224 | tf_op jit(solution)/shard_map/ppermute | solution.py:13
  434.6 38.3 %collective-permute-start.4 = (bf16[4,128,128]{2,1,0:T(8,128)(2,1)}, bf16[4,128,128]{2,1,0:T(8,128)(2,1)}, u32[]{:S(2)}, u32[]{:S(2)}) collective-permute-start(bf16[4,128,128]{2,1,0:T(8,128)(2,1)} %get-tuple-element.70), channel_id=1, source_target_pairs={{0,8},{4,12},{8,16},{12,20},{16,24},{20,28},{24,32},{28,36},{32,40... | collective-permute-start | bytes 393224 | tf_op jit(solution)/shard_map/ppermute | solution.py:13
  436.5 36.4 %collective-permute-start.5 = (bf16[4,128,128]{2,1,0:T(8,128)(2,1)}, bf16[4,128,128]{2,1,0:T(8,128)(2,1)}, u32[]{:S(2)}, u32[]{:S(2)}) collective-permute-start(bf16[4,128,128]{2,1,0:T(8,128)(2,1)} %get-tuple-element.70), channel_id=1, source_target_pairs={{0,12},{4,16},{8,20},{12,24},{16,28},{20,32},{24,36},{28,40},{32,4... | collective-permute-start | bytes 393224 | tf_op jit(solution)/shard_map/ppermute | solution.py:13
  457.1 12.2 %copy-start.49 = (bf16[8,1,128]{2,1,0:T(2,128)(2,1)S(1)}, bf16[8,1,128]{2,1,0:T(2,128)(2,1)}, u32[]{:S(2)}) copy-start(bf16[8,1,128]{2,1,0:T(2,128)(2,1)} %get-tuple-element.107) | copy-start | bytes 6148
  457.1 12.2 %copy-start.50 = (bf16[8,1,128]{2,1,0:T(2,128)(2,1)S(1)}, bf16[8,1,128]{2,1,0:T(2,128)(2,1)}, u32[]{:S(2)}) copy-start(bf16[8,1,128]{2,1,0:T(2,128)(2,1)} %get-tuple-element.111) | copy-start | bytes 6148
  461.7 18.5 %copy-start.33 = (f32[4,512]{1,0:T(4,128)}, f32[4,512]{1,0:T(4,128)S(1)}, u32[]{:S(2)}) copy-start(f32[4,512]{1,0:T(4,128)S(1)} %select_add_fusion) | copy-start | bytes 24580
  461.7 13.2 %copy-start.47 = (f32[4,128]{1,0:T(4,128)S(1)}, f32[4,128]{1,0:T(4,128)}, u32[]{:S(2)}) copy-start(f32[4,128]{1,0:T(4,128)} %copy-done.46) | copy-start | bytes 6148
  480.2 8.4 copy-start.41
  480.2 8.4 copy-start.43
  494.6 461.8 %reduce-scatter.5.cloned.1.call-start = ((), (), s32[]{:S(2)}) async-start(), calls=%async_computation.2 | async-start | bytes 5242880 | tf_op jit(solution)/shard_map/reduce_scatter | solution.py:160
  500.7 10.2 %copy-start.65 = (f32[4,128]{1,0:T(4,128)}, f32[4,128]{1,0:T(4,128)S(1)}, u32[]{:S(2)}) copy-start(f32[4,128]{1,0:T(4,128)S(1)} %pad_maximum_fusion.15) | copy-start | bytes 6148
  503.1 30.2 %collective-permute-start.10 = (f32[4,128,128]{2,1,0:T(8,128)}, f32[4,128,128]{2,1,0:T(8,128)}, u32[]{:S(2)}, u32[]{:S(2)}) collective-permute-start(f32[4,128,128]{2,1,0:T(8,128)} %get-tuple-element.46), channel_id=1, source_target_pairs={{8,0},{12,4},{16,8},{20,12},{24,16},{28,20},{32,24},{36,28},{40,32... | collective-permute-start | bytes 786440 | tf_op jit(solution)/shard_map/ppermute | solution.py:13
  504.4 35.1 %collective-permute-start.11 = (f32[4,128,128]{2,1,0:T(8,128)}, f32[4,128,128]{2,1,0:T(8,128)}, u32[]{:S(2)}, u32[]{:S(2)}) collective-permute-start(f32[4,128,128]{2,1,0:T(8,128)} %get-tuple-element.45), channel_id=1, source_target_pairs={{12,0},{16,4},{20,8},{24,12},{28,16},{32,20},{36,24},{40,28},{44,3... | collective-permute-start | bytes 786440 | tf_op jit(solution)/shard_map/ppermute | solution.py:13
  505.8 33.7 %collective-permute-start.9 = (f32[4,128,128]{2,1,0:T(8,128)}, f32[4,128,128]{2,1,0:T(8,128)}, u32[]{:S(2)}, u32[]{:S(2)}) collective-permute-start(f32[4,128,128]{2,1,0:T(8,128)} %get-tuple-element.44), channel_id=1, source_target_pairs={{4,0},{8,4},{12,8},{16,12},{20,16},{24,20},{28,24},{32,28},{36,32}... | collective-permute-start | bytes 786440 | tf_op jit(solution)/shard_map/ppermute | solution.py:13
  521.8 12.7 %copy-start.3 = (bf16[4,512,512]{1,2,0:T(8,128)(2,1)}, bf16[4,512,512]{1,2,0:T(8,128)(2,1)S(1)}, u32[]{:S(2)}) copy-start(bf16[4,512,512]{1,2,0:T(8,128)(2,1)S(1)} %multiply_convert_fusion) | copy-start | bytes 6291460
  522.1 19.1 %collective-permute-start.6 = (f32[4,128,128]{1,2,0:T(8,128)}, f32[4,128,128]{1,2,0:T(8,128)S(1)}, u32[]{:S(2)}, u32[]{:S(2)}) collective-permute-start(f32[4,128,128]{1,2,0:T(8,128)} %bitcast.76), channel_id=1, source_target_pairs={{4,0},{8,4},{12,8},{16,12},{20,16},{24,20},{28,24},{32,28},{36,32}... | collective-permute-start | bytes 786440 | tf_op jit(solution)/shard_map/ppermute | solution.py:13
  523.4 17.8 %collective-permute-start.7 = (f32[4,128,128]{1,2,0:T(8,128)}, f32[4,128,128]{1,2,0:T(8,128)}, u32[]{:S(2)}, u32[]{:S(2)}) collective-permute-start(f32[4,128,128]{1,2,0:T(8,128)} %bitcast.77), channel_id=1, source_target_pairs={{8,0},{12,4},{16,8},{20,12},{24,16},{28,20},{32,24},{36,28},{40,32... | collective-permute-start | bytes 786440 | tf_op jit(solution)/shard_map/ppermute | solution.py:13
  533.2 12.6 %collective-permute-start.8 = (f32[4,128,128]{1,2,0:T(8,128)}, f32[4,128,128]{1,2,0:T(8,128)}, u32[]{:S(2)}, u32[]{:S(2)}) collective-permute-start(f32[4,128,128]{1,2,0:T(8,128)} %bitcast.368), channel_id=1, source_target_pairs={{12,0},{16,4},{20,8},{24,12},{28,16},{32,20},{36,24},{40,28},{44,3... | collective-permute-start | bytes 786440 | tf_op jit(solution)/shard_map/ppermute | solution.py:13
  537.4 8.5 copy-start.12
  870.4 88.2 %copy-start.1 = (bf16[512,2048]{1,0:T(8,128)(2,1)S(1)}, bf16[512,2048]{1,0:T(8,128)(2,1)}, u32[]{:S(2)}) copy-start(bf16[512,2048]{1,0:T(8,128)(2,1)} %param.9) | copy-start | bytes 6291460
  (49 other events, 216.9 us)
Sparse Core Ops, SparseCore 0:
  52.0 32.5 all-gather.1
  494.8 368.8 reduce-scatter.6
  866.4 90.0 reduce-scatter.4
where the time goes:
time: 968 us; the launch traced here: 965 us
  waiting for transfers between devices  399 us (41%)
  blocking collectives  322 us (33%)
  local copies, waits for them, and re-layouts  117 us (12%)
  matrix products  43.1 us (4%)
  starting transfers between devices  31.7 us (3%)
  between operations  30 us (3%)
  other arithmetic  21.5 us (2%)
    unnamed x4, waiting for transfers between devices  315 us
    all_gather x1, blocking collectives, local(): lax.all_gather(far_key_own, 'seq', axis=1, tiled=True)  163 us
    all_gather x1, blocking collectives, local(): lax.all_gather(far_value_own, 'seq', axis=1, tiled=True)  160 us
    reduce_scatter x1, waiting for transfers between devices, local(): lax.psum_scatter(partial_out, 'mp', scatter_dimension=1, tiled=True)  79.4 us
    ppermute x12, starting transfers between devices, passed_along(): return lax.ppermute(array, axis, pairs)  31.6 us
    dynamic_slice x40, local copies, waits for them, and re-layouts, pick_rows(): lax.dynamic_index_in_dim(shaped[head_index], offsets[head_index], 1, keep...  28.4 us
    unnamed x174, local copies, waits for them, and re-layouts  27.2 us
    broadcast_in_dim x28, local copies, waits for them, and re-layouts, place_rows(): spread = jnp.where(chosen, values[:, :, None], filler)  27.1 us
  transfers between devices with their start and end apart: 15, of which 3 were waited for; matrix products, arithmetic and copies ran while one was open for 12% of the time, Pallas kernels for 0%

commit v1 on v0

v1 whole, which is shorter than its diff:
```python
import functools

import jax
import jax.numpy as jnp
from jax import lax
from jax.experimental import pallas as pl
from jax.experimental.pallas import tpu as pltpu
from jax.sharding import PartitionSpec as P

MESH = pl.DeviceIdType.MESH
BF = jnp.bfloat16
F32 = jnp.float32
HD = 128
HEADS = 4
ROWS = 512
SCALE = HD ** (-0.5)
NY, NZ = 4, 8
NEG = -1e30


def nn(a, b):
    return lax.dot_general(a, b, (((1,), (0,)), ((), ())), preferred_element_type=F32)


def nt(a, b):
    return lax.dot_general(a, b, (((1,), (1,)), ((), ())), preferred_element_type=F32)


def tn(a, b):
    return lax.dot_general(a, b, (((0,), (0,)), ((), ())), preferred_element_type=F32)


def iota(shape, dim):
    return lax.broadcasted_iota(jnp.int32, shape, dim)


def low(x):
    return x.astype(BF)


def hi_lo(x):
    hi = x.astype(BF).astype(F32)
    return hi, x - hi


def kernel(offs, q, k, v, w, g, mixed, dq, dk, dv,
           gbuf, gacc, dot_, do_, nkv, fown, fx, fkv, e_l, e_n, e_f, o_l, o_n, o_f,
           st_l, st_n, st_f, q_n, q_f, a_n, a_f, att, c_l, c_n, c_f, inn, dqt, dka, dva,
           fgr, rz, ry, xs, xr, ng, nrb, mcs, mcr, mkeep, mxs, mxr,
           ss, rs, nss, nrs, gss, grs):
    s = lax.axis_index("seq")
    m = lax.axis_index("mp")
    y, z, xh = s // 16, (s // 2) % NZ, s % 2
    l, c = m // 2, m % 2
    pos = s % 4

    def dev(yy, zz, hh):
        return ((yy * NZ + zz) * 2 + hh, m)

    core = (s, l * 2 + 1 - c)
    across = (s, (1 - l) * 2 + c)
    xpart = dev(y, z, 1 - xh)
    zup = dev(y, (z + 1) % NZ, xh)
    zdn = dev(y, (z + NZ - 1) % NZ, xh)
    yps = [dev((y + d) % NY, z, xh) for d in range(1, NY)]
    diag = dev(y, z + 1 - 2 * (z % 2), 1 - xh)
    partners = [core, across, xpart, zup, zdn, diag] + yps

    barrier = pltpu.get_barrier_semaphore()
    for p in partners:
        pl.semaphore_signal(barrier, inc=1, device_id=p, device_id_type=MESH)

    def rc(src, dst, i, to):
        return pltpu.make_async_remote_copy(
            src_ref=src, dst_ref=dst, send_sem=ss.at[i], recv_sem=rs.at[i],
            device_id=to, device_id_type=MESH)

    def hc(h):
        return pl.ds(h * HD, HD)

    ia = iota((HD, ROWS), 0)
    ii = iota((HD, ROWS), 1)
    for h in range(HEADS):
        far = jnp.where((ii == 64 * ia + offs[1, h]) & (ia < 8), 1.0, 0.0).astype(BF)
        a_f[h] = far
        few = far[:16]
        fk = nn(few, k[:, hc(h)])
        fv = nn(few, v[:, hc(h)])
        fown[:, hc(h)] = low(jnp.concatenate([fk[:8], fv[:8]], 0))
    pl.semaphore_wait(barrier, len(partners))

    cx = rc(fown, fx, 0, xpart)
    cx.start()
    cg_core = rc(g, gbuf.at[0], 1, core)
    cg_x = rc(g, gbuf.at[1], 2, across)
    cg_x.start()
    cg_core.start()

    for h in range(HEADS):
        near = jnp.where(ii == 4 * ia + offs[0, h], 1.0, 0.0).astype(BF)
        a_n[h] = near
        nkv[pos, 0:128, hc(h)] = low(nn(near, k[:, hc(h)]))
        nkv[pos, 128:256, hc(h)] = low(nn(near, v[:, hc(h)]))
    for t in range(1, 4):
        @pl.when(t > pos)
        def _():
            nkv[t] = jnp.zeros((256, ROWS), BF)

    def near_copy(t):
        return pltpu.make_async_remote_copy(
            src_ref=nkv.at[pos], dst_ref=nkv.at[pos], send_sem=nss.at[t],
            recv_sem=nrs.at[pos], device_id=(s - pos + t, m), device_id_type=MESH)

    def near_recv(t):
        return pltpu.make_async_remote_copy(
            src_ref=nkv.at[t], dst_ref=nkv.at[t], send_sem=nss.at[t],
            recv_sem=nrs.at[t], device_id=(s - pos + t, m), device_id_type=MESH)

    for t in range(1, 4):
        @pl.when(t > pos)
        def _():
            near_copy(t).start()

    def local_fwd(h):
        for ib in range(2):
            nk = 256 * (ib + 1)
            qs = slice(ib * 256, ib * 256 + 256)
            st = nt(k[0:nk, hc(h)], q[qs, hc(h)]) * SCALE
            jj = iota((nk, 256), 0)
            qq = iota((nk, 256), 1) + ib * 256
            st = jnp.where(jj <= qq, st, NEG)
            mx = jnp.max(st, 0, keepdims=True).astype(BF).astype(F32)
            e = jnp.exp(st - mx)
            el = low(e)
            e_l[h, 0:nk, qs] = el
            o_l[h, :, qs] = tn(v[0:nk, hc(h)], el)
            st_l[h, 0:1, qs] = mx
            st_l[h, 1:2, qs] = jnp.sum(e, 0, keepdims=True)

    local_fwd(0)
    cx.wait()
    mine = fown[...].astype(F32)
    other = fx[...].astype(F32)
    first = jnp.where(xh == 0, mine, other)
    second = jnp.where(xh == 0, other, mine)
    fkv[z, y] = low(jnp.concatenate([first[:8], second[:8], first[8:], second[8:]], 0))
    cy = [rc(fkv.at[z, y], fkv.at[z, y], 4 + d, yps[d]) for d in range(3)]
    for cp in cy:
        cp.start()
    local_fwd(1)
    for cp in cy:
        cp.wait()

    def z_step(t):
        up = (z + NZ - t) % NZ
        dn = (z + t) % NZ
        if t < 3:
            a, b = fkv.at[up], fkv.at[dn]
        else:
            a, b = fkv.at[up, pl.ds(0, 2)], fkv.at[dn, pl.ds(2, 2)]
        return rc(a, a, 8 + t, zup), rc(b, b, 12 + t, zdn)

    zs = [z_step(t) for t in range(4)]

    def z_go(t):
        if t:
            zs[t - 1][0].wait_recv()
            zs[t - 1][1].wait_recv()
        if t < 4:
            zs[t][0].start()
            zs[t][1].start()

    def grad_part(slot):
        src = [(l, c), (l, 1 - c), (1 - l, c), (1 - l, 1 - c)][slot]
        cols = pl.ds(pl.multiple_of((src[0] * 2 + src[1]) * ROWS, ROWS), ROWS)
        part = nt(w[:, cols], g[...] if slot == 0 else gbuf[slot - 1])
        if slot:
            part = part + gacc[...]
        gacc[...] = part

    z_go(0)
    local_fwd(2)
    z_go(1)
    local_fwd(3)
    cg_core.wait()
    grad_part(0)
    z_go(2)
    grad_part(1)
    z_go(3)
    cg_x.wait()
    cg_f = rc(gbuf.at[1], gbuf.at[2], 3, core)
    cg_f.start()
    grad_part(2)
    cg_f.wait()
    grad_part(3)
    dot_[...] = low(gacc[...])
    do_[...] = low(gacc[...].T)

    def level_fwd(h, sel, kk, vv, seen, e_s, o_s, st_s, q_s):
        qq = low(nn(sel, q[:, hc(h)]))
        q_s[h] = qq
        st = nt(kk, qq) * SCALE
        st = jnp.where(seen, st, NEG)
        mx = jnp.max(st, 0, keepdims=True).astype(BF).astype(F32)
        e = jnp.exp(st - mx)
        el = low(e)
        e_s[h] = el
        o_s[h] = tn(vv, el)
        st_s[h, 0:1, :] = mx
        st_s[h, 1:2, :] = jnp.sum(e, 0, keepdims=True)

    jn = iota((ROWS, HD), 0)
    an = iota((ROWS, HD), 1)
    near_seen = jn <= pos * 128 + an
    key_index = ((jn // 16) % 4) * 128 + (jn // 64) * 16 + jn % 16
    far_seen = key_index <= s * 8 + an

    def near_k(h):
        return nkv[:, 0:128, hc(h)].reshape(ROWS, HD)

    def near_v(h):
        return nkv[:, 128:256, hc(h)].reshape(ROWS, HD)

    def far_k(h):
        return fkv[:, :, 0:16, hc(h)].reshape(ROWS, HD)

    def far_v(h):
        return fkv[:, :, 16:32, hc(h)].reshape(ROWS, HD)

    for t in range(3):
        @pl.when(t < pos)
        def _():
            near_recv(t).wait_recv()
    for h in range(HEADS):
        level_fwd(h, a_n[h], near_k(h), near_v(h), near_seen, e_n, o_n, st_n, q_n)
    z_go(4)
    for h in range(HEADS):
        level_fwd(h, a_f[h], far_k(h), far_v(h), far_seen, e_f, o_f, st_f, q_f)

    lane = iota((1, ROWS), 1)

    def spread(o_s, st_s, sel, h):
        top = st_s[h, 0:1, :]
        hi, lo = hi_lo(st_s[h, 1:2, :])
        rest = jnp.concatenate([top, hi, lo, jnp.zeros((13, HD), F32)], 0)
        both = nn(low(jnp.concatenate([o_s[h], rest], 0)), sel)
        return both[0:HD], both[HD:HD + 1], both[HD + 1:HD + 2] + both[HD + 2:HD + 3]

    def picked(cf, inner, sel):
        c_hi, c_lo = hi_lo(cf)
        i_hi, i_lo = hi_lo(inner)
        rows = jnp.concatenate([c_hi, c_lo, i_hi, i_lo, jnp.zeros((12, ROWS), F32)], 0)
        got = nt(low(rows), sel)
        return got[0:1] + got[1:2], got[2:3] + got[3:4]

    def combine(h):
        on, mn, sn = spread(o_n, st_n, a_n[h], h)
        of, mf, sf = spread(o_f, st_f, a_f[h], h)
        is_n = lane % 4 == offs[0, h]
        is_f = lane % 64 == offs[1, h]
        mn = jnp.where(is_n, mn, NEG)
        mf = jnp.where(is_f, mf, NEG)
        ml = st_l[h, 0:1, :]
        top = jnp.maximum(ml, jnp.maximum(mn, mf))
        wl, wn, wf = jnp.exp(ml - top), jnp.exp(mn - top), jnp.exp(mf - top)
        total = st_l[h, 1:2, :] * wl + sn * wn + sf * wf
        inv = 1.0 / total
        out = low((o_l[h] * wl + on * wn + of * wf) * inv)
        att[hc(h), :] = out
        inner = jnp.sum(dot_[hc(h), :].astype(F32) * out.astype(F32), 0, keepdims=True)
        c_l[h, 0:1, :] = wl * inv
        inn[h, 0:1, :] = inner
        cn, inner_n = picked(wn * inv, inner, a_n[h])
        cf, inner_f = picked(wf * inv, inner, a_f[h])
        c_n[h, 0:1, :] = cn
        c_n[h, 1:2, :] = inner_n
        c_f[h, 0:1, :] = cf
        c_f[h, 1:2, :] = inner_f

    for h in range(HEADS):
        combine(h)

    def level_bwd(h, sel, kk, vv, e_s, q_s, c_s):
        dd = low(nn(sel, do_[:, hc(h)]))
        prob = e_s[h].astype(F32) * c_s[h, 0:1, :]
        ds = low(prob * (nt(vv, dd) - c_s[h, 1:2, :]))
        return low(nn(ds, q_s[h]) * SCALE), low(nn(low(prob), dd)), nn(low(tn(kk, ds) * SCALE), sel)

    for h in range(HEADS):
        kt, vt, qt = level_bwd(h, a_f[h], far_k(h), far_v(h), e_f, q_f, c_f)
        fgr[:, :, 0:16, hc(h)] = kt.reshape(NZ, NY, 16, HD)
        fgr[:, :, 16:32, hc(h)] = vt.reshape(NZ, NY, 16, HD)
        dqt[h] = qt

    def rz_step(t):
        up = (z + 4 - t) % NZ
        dn = (z + 4 + t) % NZ
        if t:
            return (rc(fgr.at[up], rz.at[0, t], 16 + t, zup), rc(fgr.at[dn], rz.at[1, t], 20 + t, zdn))
        return (rc(fgr.at[up, pl.ds(0, 2)], rz.at[0, 0, pl.ds(0, 2)], 16, zup),
                rc(fgr.at[dn, pl.ds(2, 2)], rz.at[1, 0, pl.ds(2, 2)], 20, zdn))

    rzs = [rz_step(t) for t in range(4)]

    def add_block(dst, src):
        dst[...] = low(dst[...].astype(F32) + src[...].astype(F32))

    def rz_go(t):
        if t:
            rzs[t - 1][0].wait_recv()
            rzs[t - 1][1].wait_recv()
            up = (z + 4 - t) % NZ
            dn = (z + 4 + t) % NZ
            if t == 1:
                add_block(fgr.at[up, pl.ds(0, 2)], rz.at[0, 0, pl.ds(0, 2)])
                add_block(fgr.at[dn, pl.ds(2, 2)], rz.at[1, 0, pl.ds(2, 2)])
            elif t < 4:
                add_block(fgr.at[up], rz.at[0, t - 1])
                add_block(fgr.at[dn], rz.at[1, t - 1])
        if t < 4:
            rzs[t][0].start()
            rzs[t][1].start()

    rz_go(0)
    for h in range(HEADS):
        kt, vt, qt = level_bwd(h, a_n[h], near_k(h), near_v(h), e_n, q_n, c_n)
        ng[:, 0:128, hc(h)] = kt.reshape(4, HD, HD)
        ng[:, 128:256, hc(h)] = vt.reshape(4, HD, HD)
        dqt[h] = dqt[h] + qt

    def grad_copy(t):
        return pltpu.make_async_remote_copy(
            src_ref=ng.at[t], dst_ref=nrb.at[pos], send_sem=gss.at[t],
            recv_sem=grs.at[pos], device_id=(s - pos + t, m), device_id_type=MESH)

    def grad_recv(t):
        return pltpu.make_async_remote_copy(
            src_ref=ng.at[t], dst_ref=nrb.at[t], send_sem=gss.at[t],
            recv_sem=grs.at[t], device_id=(s - pos + t, m), device_id_type=MESH)

    for t in range(3):
        @pl.when(t < pos)
        def _():
            grad_copy(t).start()
    rz_go(1)

    def mixed_part(ll, cc):
        cols = pl.ds(pl.multiple_of((ll * 2 + cc) * ROWS, ROWS), ROWS)
        return tn(att[...], w[:, cols])

    mcs[0] = low(mixed_part(1 - l, 1 - c))
    cm0 = rc(mcs.at[0], mcr.at[0], 24, core)
    cm0.start()
    mkeep[...] = mixed_part(1 - l, c)
    cm0.wait()
    mxs[...] = low(mkeep[...] + mcr[0].astype(F32))
    cmx = rc(mxs, mxr, 25, across)
    cmx.start()
    rz_go(2)
    mcs[1] = low(mixed_part(l, 1 - c))
    cm1 = rc(mcs.at[1], mcr.at[1], 26, core)
    cm1.start()
    mkeep[...] = mixed_part(l, c)
    cm1.wait()
    mkeep[...] = mkeep[...] + mcr[1].astype(F32)

    def local_bwd(h):
        for ib in range(2):
            nk = 256 * (ib + 1)
            qs = slice(ib * 256, ib * 256 + 256)
            prob = e_l[h, 0:nk, qs].astype(F32) * c_l[h, 0:1, qs]
            dp = nn(v[0:nk, hc(h)], dot_[hc(h), qs])
            ds = low(prob * (dp - inn[h, 0:1, qs]))
            vt = nn(low(prob), do_[qs, hc(h)])
            kt = nn(ds, q[qs, hc(h)]) * SCALE
            if ib == 0:
                dva[0:nk, hc(h)] = vt
                dka[0:nk, hc(h)] = kt
            else:
                dva[0:256, hc(h)] = dva[0:256, hc(h)] + vt[0:256]
                dka[0:256, hc(h)] = dka[0:256, hc(h)] + kt[0:256]
                dva[256:512, hc(h)] = vt[256:512]
                dka[256:512, hc(h)] = kt[256:512]
            qt = tn(k[0:nk, hc(h)], ds) * SCALE + dqt[h, :, qs]
            dq[qs, hc(h)] = low(qt.T)

    local_bwd(0)
    local_bwd(1)
    rz_go(3)
    local_bwd(2)
    local_bwd(3)
    rz_go(4)
    total = fgr[z].astype(F32) + rz[0, 3].astype(F32) + rz[1, 3].astype(F32)
    fgr[z] = low(total)
    cry = [rc(fgr.at[z, (y + d + 1) % NY], ry.at[d], 28 + d, yps[d]) for d in range(3)]
    for cp in cry:
        cp.start()
    for t in range(1, 4):
        @pl.when(t > pos)
        def _():
            grad_recv(t).wait_recv()
            add_block(ng.at[pos], nrb.at[t])
    jt = iota((ROWS, HD), 0)
    at = iota((ROWS, HD), 1)
    for h in range(HEADS):
        back = jnp.where(jt == 4 * at + offs[0, h], 1.0, 0.0).astype(BF)
        dka[:, hc(h)] = dka[:, hc(h)] + nn(back, ng[pos, 0:128, hc(h)])
        dva[:, hc(h)] = dva[:, hc(h)] + nn(back, ng[pos, 128:256, hc(h)])
    for cp in cry:
        cp.wait()
    total = fgr[z, y].astype(F32)
    for d in range(3):
        total = total + ry[d].astype(F32)
    low_half = jnp.concatenate([total[0:8], total[16:24]], 0)
    high_half = jnp.concatenate([total[8:16], total[24:32]], 0)
    xs[...] = low(jnp.where(xh == 0, high_half, low_half))
    cxr = rc(xs, xr, 27, xpart)
    cxr.start()
    cmx.wait()
    mixed[...] = low(mkeep[...] + mxr[...].astype(F32))
    cxr.wait()
    far_sum = jnp.where(xh == 0, low_half, high_half) + xr[...].astype(F32)
    far_key = low(jnp.concatenate([far_sum[0:8], jnp.zeros((8, ROWS), F32)], 0))
    far_val = low(jnp.concatenate([far_sum[8:16], jnp.zeros((8, ROWS), F32)], 0))
    jf = iota((ROWS, 16), 0)
    af = iota((ROWS, 16), 1)
    for h in range(HEADS):
        back = jnp.where((jf == 64 * af + offs[1, h]) & (af < 8), 1.0, 0.0).astype(BF)
        dk[:, hc(h)] = low(dka[:, hc(h)] + nn(back, far_key[:, h * HD:(h + 1) * HD]))
        dv[:, hc(h)] = low(dva[:, hc(h)] + nn(back, far_val[:, h * HD:(h + 1) * HD]))

    for t in range(4):
        zs[t][0].wait_send()
        zs[t][1].wait_send()
        rzs[t][0].wait_send()
        rzs[t][1].wait_send()
    for t in range(1, 4):
        @pl.when(t > pos)
        def _():
            near_copy(t).wait_send()
    for t in range(3):
        @pl.when(t < pos)
        def _():
            grad_copy(t).wait_send()


def local(queries, key_rows, value_rows, out_weight, grad_out, offsets):
    vm = pl.BlockSpec(memory_space=pltpu.VMEM)
    shape = jax.ShapeDtypeStruct((ROWS, ROWS), BF)
    V = pltpu.VMEM
    dma = pltpu.SemaphoreType.DMA
    return pl.pallas_call(
        kernel,
        out_shape=(shape,) * 4,
        in_specs=[pl.BlockSpec(memory_space=pltpu.SMEM)] + [vm] * 5,
        out_specs=(vm,) * 4,
        scratch_shapes=[
            V((3, ROWS, ROWS), BF), V((ROWS, ROWS), F32), V((ROWS, ROWS), BF), V((ROWS, ROWS), BF),
            V((4, 256, ROWS), BF), V((16, ROWS), BF), V((16, ROWS), BF), V((NZ, NY, 32, ROWS), BF),
            V((HEADS, ROWS, ROWS), BF), V((HEADS, ROWS, HD), BF), V((HEADS, ROWS, HD), BF),
            V((HEADS, HD, ROWS), F32), V((HEADS, HD, HD), F32), V((HEADS, HD, HD), F32),
            V((HEADS, 8, ROWS), F32), V((HEADS, 8, HD), F32), V((HEADS, 8, HD), F32),
            V((HEADS, HD, HD), BF), V((HEADS, HD, HD), BF),
            V((HEADS, HD, ROWS), BF), V((HEADS, HD, ROWS), BF),
            V((ROWS, ROWS), BF),
            V((HEADS, 8, ROWS), F32), V((HEADS, 8, HD), F32), V((HEADS, 8, HD), F32), V((HEADS, 8, ROWS), F32),
            V((HEADS, HD, ROWS), F32), V((ROWS, ROWS), F32), V((ROWS, ROWS), F32),
            V((NZ, NY, 32, ROWS), BF), V((2, 4, NY, 32, ROWS), BF), V((3, 32, ROWS), BF),
            V((16, ROWS), BF), V((16, ROWS), BF),
            V((4, 256, ROWS), BF), V((4, 256, ROWS), BF),
            V((2, ROWS, ROWS), BF), V((2, ROWS, ROWS), BF), V((ROWS, ROWS), F32),
            V((ROWS, ROWS), BF), V((ROWS, ROWS), BF),
            dma((32,)), dma((32,)), dma((4,)), dma((4,)), dma((4,)), dma((4,)),
        ],
        compiler_params=pltpu.CompilerParams(
            collective_id=0, has_side_effects=True, vmem_limit_bytes=56 << 20),
        cost_estimate=pl.CostEstimate(flops=4_400_000_000, bytes_accessed=8 << 20, transcendentals=1_400_000),
        name="dilated",
    )(offsets, queries, key_rows, value_rows, out_weight, grad_out)


def solution(mesh):
    return jax.shard_map(
        local,
        mesh=mesh,
        in_specs=(
            P("seq", "mp"),
            P("seq", "mp"),
            P("seq", "mp"),
            P("mp", None),
            P("seq", "mp"),
            P(None, "mp"),
        ),
        out_specs=(P("seq", "mp"), P("seq", "mp"), P("seq", "mp"), P("seq", "mp")),
        check_vma=False,
    )
```

time: 968 us -> 91.9 us (0.09)
  the two profiles are of different devices: /device:TPU:1 before, /device:TPU:2 now
where the time goes in v1:
time: 91.9 us; the launch traced here: 91.8 us
  Pallas kernels  85.7 us (93%)
  local copies, waits for them, and re-layouts  5.42 us (6%)
    pallas_call x1, Pallas kernels, local(): pl.pallas_call(kernel, out_shape=(shape,) * 4, in_specs=[pl.BlockSpec(mem...  85.7 us
    unnamed x8, local copies, waits for them, and re-layouts  5.42 us

profile of v1, /device:TPU:2, one launch (start us, length us, event | category | flops | bytes accessed | tf_op | source)
XLA Modules:
  0.0 91.8 jit_solution(13455383901364833329)
XLA Ops:
  0.6 85.7 %dilated.1 = (bf16[512,512]{1,0:T(8,128)(2,1)}, bf16[512,512]{1,0:T(8,128)(2,1)}, bf16[512,512]{1,0:T(8,128)(2,1)}, bf16[512,512]{1,0:T(8,128)(2,1)}) custom-call(s32[2,4]{1,0:T(2,128)} %offs.1, bf16[512,512]{1,0:T(8,128)(2,1)} %q.1, bf16[512,512]{1,0:T(8,128)(2,1)} %k.1, bf16[512,512]{1,0:T(8,128)(2,1)} %v.1, bf16[512,2048]{1,0:T(8,128)(2,1)} %w.1, ...), custom_call_target="tpu_custom_call" | custom-call | flops 4400000000 | bytes 8388608 | tf_op jit(solution)/shard_map/dilated/pallas_call | solution.py:452
  86.3 0.0 copy-start.1
  86.4 0.0 copy-start
  86.4 2.0 %copy.14 = bf16[512,512]{1,0:T(8,128)(2,1)} copy(bf16[512,512]{1,0:T(8,128)(2,1)} %get-tuple-element.8) | data formatting | bytes 1048576
  88.3 1.9 %copy.15 = bf16[512,512]{1,0:T(8,128)(2,1)} copy(bf16[512,512]{1,0:T(8,128)(2,1)} %get-tuple-element.9) | data formatting | bytes 1048576
  90.2 0.0 copy-done.1
  90.2 0.8 copy.16
  91.0 0.0 copy-done
  91.0 0.8 copy.17
Async XLA Ops:
  86.3 3.8 %copy-start.1 = (bf16[512,512]{1,0:T(8,128)(2,1)S(1)}, bf16[512,512]{1,0:T(8,128)(2,1)}, u32[]{:S(2)}) copy-start(bf16[512,512]{1,0:T(8,128)(2,1)} %get-tuple-element.10) | copy-start | bytes 1572868
  86.4 4.6 %copy-start = (bf16[512,512]{1,0:T(8,128)(2,1)S(1)}, bf16[512,512]{1,0:T(8,128)(2,1)}, u32[]{:S(2)}) copy-start(bf16[512,512]{1,0:T(8,128)(2,1)} %get-tuple-element.11) | copy-start | bytes 1572868

commit v2 on v1

v2 whole, which is shorter than its diff:
```python
import functools

import jax
import jax.numpy as jnp
from jax import lax
from jax.experimental import pallas as pl
from jax.experimental.pallas import tpu as pltpu
from jax.sharding import PartitionSpec as P

MESH = pl.DeviceIdType.MESH
BF = jnp.bfloat16
F32 = jnp.float32
HD = 128
HEADS = 4
ROWS = 512
SCALE = HD ** (-0.5)
NY, NZ = 4, 8
NEG = -1e30


def nn(a, b):
    return lax.dot_general(a, b, (((1,), (0,)), ((), ())), preferred_element_type=F32)


def nt(a, b):
    return lax.dot_general(a, b, (((1,), (1,)), ((), ())), preferred_element_type=F32)


def tn(a, b):
    return lax.dot_general(a, b, (((0,), (0,)), ((), ())), preferred_element_type=F32)


def iota(shape, dim):
    return lax.broadcasted_iota(jnp.int32, shape, dim)


def low(x):
    return x.astype(BF)


def hi_lo(x):
    hi = x.astype(BF).astype(F32)
    return hi, x - hi


def kernel(offs, qh, kh, vh, wh, gh, mixed, dq, dk, dv,
           q, k, v, w, g, gbuf, gacc, dot_, do_, nkv, e_l, e_n, e_f, o_l, o_n,
           st_l, st_n, q_n, a_n, a_f, f16, att, c_l, c_n, inn, dqt, dqa, dka, dva,
           p1s, p1r, fkv, fo, p5s, p5r, fgr, rz, p8s, p8r,
           ng, nrb, mcs, mcr, mkeep, mxs, mxr,
           ins, ss, rs):
    s = lax.axis_index("seq")
    m = lax.axis_index("mp")
    y, z, xh = s // 16, (s // 2) % NZ, s % 2
    l, c = m // 2, m % 2
    pos = s % 4

    def dev(yy, zz, hh):
        return ((yy * NZ + zz) * 2 + hh, m)

    core = (s, l * 2 + 1 - c)
    across = (s, (1 - l) * 2 + c)
    xpart = dev(y, z, 1 - xh)
    zpart = dev(y, z + 1 - 2 * (z % 2), xh)
    ys = [(y + d) % NY for d in range(1, NY)]
    yps = [dev(yy, z, xh) for yy in ys]
    zps = [dev(y, (z + d) % NZ, xh) for d in range(1, NZ)]
    yx = [((y + n // 2) % NY, (xh + n % 2) % 2) for n in range(1, 2 * NY)]
    partners = [core, across] + [dev(yy, z, hh) for yy, hh in yx] + zps

    barrier = pltpu.get_barrier_semaphore()
    for p in partners:
        pl.semaphore_signal(barrier, inc=1, device_id=p, device_id_type=MESH)
    loads = [pltpu.make_async_copy(a, b, ins.at[i])
             for i, (a, b) in enumerate([(kh, k), (vh, v), (qh, q), (gh, g), (wh, w)])]
    for cp in loads:
        cp.start()

    def rc(src, dst, i, to):
        return pltpu.make_async_remote_copy(
            src_ref=src, dst_ref=dst, send_sem=ss.at[i], recv_sem=rs.at[i],
            device_id=to, device_id_type=MESH)

    def hc(h):
        return pl.ds(h * HD, HD)

    ia = iota((HD, ROWS), 0)
    ii = iota((HD, ROWS), 1)
    for h in range(HEADS):
        a_n[h] = jnp.where(ii == 4 * ia + offs[0, h], 1.0, 0.0).astype(BF)
        fa = ia - 8 * y
        a_f[h] = jnp.where((ii == 64 * fa + offs[1, h]) & (fa >= 0) & (fa < 8), 1.0, 0.0).astype(BF)
        f16[h] = jnp.where((ii[:16] == 64 * ia[:16] + offs[1, h]) & (ia[:16] < 8), 1.0, 0.0).astype(BF)
    for cp in loads[:3]:
        cp.wait()
    pad8 = jnp.zeros((8, HD), F32)
    for h in range(HEADS):
        rows = [nn(f16[h], x[:, hc(h)])[:8] for x in (k, v, q)]
        p1s[h] = low(jnp.concatenate(rows + [pad8], 0))
    for h in range(HEADS):
        nkv[pos, 0:128, hc(h)] = low(nn(a_n[h], k[:, hc(h)]))
        nkv[pos, 128:256, hc(h)] = low(nn(a_n[h], v[:, hc(h)]))
    for t in range(1, 4):
        @pl.when(t > pos)
        def _():
            nkv[t] = jnp.zeros((256, ROWS), BF)

    def near_send(base, slot, to):
        return [rc(nkv.at[slot, pl.ds(128 * n, 128)], nkv.at[slot, pl.ds(128 * n, 128)], base + n, to)
                for n in range(2)]

    z_even = z % 2 == 0
    near_z = near_send(40, pos, zpart)
    near_x = near_send(42, pos, xpart)
    relay_z = near_send(44, 0, zpart)
    relay_x = near_send(44, 1, xpart)

    def local_fwd(h):
        for ib in range(2):
            nk = 256 * (ib + 1)
            qs = slice(ib * 256, ib * 256 + 256)
            st = nt(k[0:nk, hc(h)], q[qs, hc(h)]) * SCALE
            jj = iota((nk, 256), 0)
            qq = iota((nk, 256), 1) + ib * 256
            st = jnp.where(jj <= qq, st, NEG)
            mx = jnp.max(st, 0, keepdims=True).astype(BF).astype(F32)
            e = jnp.exp(st - mx)
            el = low(e)
            e_l[h, 0:nk, qs] = el
            o_l[h, :, qs] = tn(v[0:nk, hc(h)], el)
            st_l[h, 0:1, qs] = mx
            st_l[h, 1:2, qs] = jnp.sum(e, 0, keepdims=True)

    local_fwd(0)
    local_fwd(1)
    loads[3].wait()
    pl.semaphore_wait(barrier, len(partners))

    p1 = [rc(p1s.at[yx[n][0]], p1r.at[xh, y], n, dev(yx[n][0], z, yx[n][1])) for n in range(7)]
    for cp in p1:
        cp.start()
    p1r[xh, y] = p1s[y]

    @pl.when(xh == 0)
    def _():
        for cp in near_x:
            cp.start()

    @pl.when(z_even)
    def _():
        for cp in near_z:
            cp.start()

    def halves(src, dst, base, to):
        return [rc(src.at[pl.ds(256 * n, 256)], dst.at[pl.ds(256 * n, 256)], base + n, to) for n in range(2)]

    cg_x = halves(g, gbuf.at[1], 50, across)
    cg_core = rc(g, gbuf.at[0], 28, core)
    cg_f = halves(gbuf.at[1], gbuf.at[2], 52, core)
    for cp in cg_x:
        cp.start()
    cg_core.start()
    local_fwd(2)
    local_fwd(3)
    for cp in p1:
        cp.wait()
    for hh in range(2):
        got = [p1r[hh, t].astype(F32) for t in range(NY)]
        fkv[z, hh] = low(jnp.concatenate([x[0:8] for x in got] + [x[8:16] for x in got], 0))
    p3 = [rc(fkv.at[z], fkv.at[z], 7 + d, zps[d]) for d in range(7)]
    for d in (3, 2, 4, 1, 5, 0, 6):
        p3[d].start()
    got = [p1r[xh, t].astype(F32) for t in range(NY)]
    fq = low(jnp.concatenate([x[16:24] for x in got] + [jnp.zeros((96, HD), F32)], 0))

    def grad_part(slot):
        src = [(l, c), (l, 1 - c), (1 - l, c), (1 - l, 1 - c)][slot]
        cols = pl.ds(pl.multiple_of((src[0] * 2 + src[1]) * ROWS, ROWS), ROWS)
        part = nt(w[:, cols], g[...] if slot == 0 else gbuf[slot - 1])
        if slot:
            part = part + gacc[...]
        gacc[...] = part

    loads[4].wait()
    grad_part(0)
    cg_core.wait()
    grad_part(1)

    @pl.when(pos == 1)
    def _():
        for n in range(2):
            near_x[n].wait_recv()
            relay_z[n].start()

    @pl.when(pos == 3)
    def _():
        for n in range(2):
            near_z[n].wait_recv()
            relay_x[n].start()

    def scores(kk, qq, vv, seen):
        st = nt(kk, qq) * SCALE
        st = jnp.where(seen, st, NEG)
        mx = jnp.max(st, 0, keepdims=True).astype(BF).astype(F32)
        e = jnp.exp(st - mx)
        el = low(e)
        hi, lo = hi_lo(jnp.sum(e, 0, keepdims=True))
        return el, low(jnp.concatenate([tn(vv, el), mx, hi, lo, jnp.zeros((13, HD), F32)], 0))

    jn = iota((ROWS, HD), 0)
    an = iota((ROWS, HD), 1)
    near_seen = jn <= pos * 128 + an
    key_index = ((jn // 8) % 4) * 128 + (jn // 64) * 16 + ((jn // 32) % 2) * 8 + jn % 8
    query_index = (an // 8) * 128 + z * 16 + xh * 8 + an % 8
    far_seen = key_index <= query_index

    def near_k(h):
        return nkv[:, 0:128, hc(h)].reshape(ROWS, HD)

    def near_v(h):
        return nkv[:, 128:256, hc(h)].reshape(ROWS, HD)

    for cp in p3:
        cp.wait_recv()
    far_k = fkv[:, :, 0:32, :].reshape(ROWS, HD)
    far_v = fkv[:, :, 32:64, :].reshape(ROWS, HD)
    el, block = scores(far_k, fq, far_v, far_seen)
    e_f[...] = el
    fo[y] = block
    p4 = [rc(fo.at[y], fo.at[y], 14 + d, yps[d]) for d in range(3)]
    for cp in p4:
        cp.start()

    for n in range(2):
        cg_x[n].wait()
        cg_f[n].start()
    grad_part(2)
    for n in range(2):
        cg_f[n].wait()
    grad_part(3)
    dot_[...] = low(gacc[...])
    do_[...] = low(gacc[...].T)

    @pl.when(pos == 2)
    def _():
        for n in range(2):
            near_z[n].wait_recv()
            relay_x[n].wait_recv()

    @pl.when(pos == 3)
    def _():
        for n in range(2):
            near_x[n].wait_recv()
            relay_z[n].wait_recv()

    for h in range(HEADS):
        qq = low(nn(a_n[h], q[:, hc(h)]))
        q_n[h] = qq
        el, block = scores(near_k(h), qq, near_v(h), near_seen)
        e_n[h] = el
        o_n[h] = block

    lane = iota((1, ROWS), 1)

    def spread(block, sel):
        both = nn(block, sel)
        return both[0:HD], both[HD:HD + 1], both[HD + 1:HD + 2] + both[HD + 2:HD + 3]

    def picked(cf, inner, sel):
        c_hi, c_lo = hi_lo(cf)
        i_hi, i_lo = hi_lo(inner)
        rows = jnp.concatenate([c_hi, c_lo, i_hi, i_lo, jnp.zeros((12, ROWS), F32)], 0)
        return nt(low(rows), sel)

    def combine(h):
        on, mn, sn = spread(o_n[h], a_n[h])
        of, mf, sf = spread(fo[h], a_f[h])
        mn = jnp.where(lane % 4 == offs[0, h], mn, NEG)
        mf = jnp.where(lane % 64 == offs[1, h], mf, NEG)
        ml = st_l[h, 0:1, :]
        top = jnp.maximum(ml, jnp.maximum(mn, mf))
        wl, wn, wf = jnp.exp(ml - top), jnp.exp(mn - top), jnp.exp(mf - top)
        total = st_l[h, 1:2, :] * wl + sn * wn + sf * wf
        inv = 1.0 / total
        out = low((o_l[h] * wl + on * wn + of * wf) * inv)
        att[hc(h), :] = out
        inner = jnp.sum(dot_[hc(h), :].astype(F32) * out.astype(F32), 0, keepdims=True)
        c_l[h, 0:1, :] = wl * inv
        inn[h, 0:1, :] = inner
        far = picked(wf * inv, inner, a_f[h])
        p5s[h] = low(jnp.concatenate([nn(f16[h], do_[:, hc(h)])[:8], far[:8]], 0))
        c_n[h] = picked(wn * inv, inner, a_n[h])

    for cp in p4:
        cp.wait()
    for h in range(HEADS):
        combine(h)
    p5 = [rc(p5s.at[ys[d]], p5r.at[y], 17 + d, yps[d]) for d in range(3)]
    for cp in p5:
        cp.start()
    p5r[y] = p5s[y]

    def mixed_part(ll, cc, n):
        cols = pl.ds(pl.multiple_of((ll * 2 + cc) * ROWS, ROWS), ROWS)
        return tn(att[:, 256 * n:256 * n + 256], w[:, cols])

    def half(n):
        return pl.ds(256 * n, 256)

    cm0 = halves(mcs.at[0], mcr.at[0], 54, core)
    cm1 = halves(mcs.at[1], mcr.at[1], 56, core)
    cmx = halves(mxs, mxr, 58, across)
    for n in range(2):
        mcs[0, half(n), :] = low(mixed_part(1 - l, 1 - c, n))
        cm0[n].start()
    for n in range(2):
        part = mixed_part(1 - l, c, n)
        cm0[n].wait()
        mxs[half(n), :] = low(part + mcr[0, half(n), :].astype(F32))
        cmx[n].start()

    for cp in p5:
        cp.wait()
    got = [p5r[t].astype(F32) for t in range(NY)]
    fd = low(jnp.concatenate([x[0:8] for x in got] + [jnp.zeros((96, HD), F32)], 0))
    stat = got[0][8:16] + got[1][8:16] + got[2][8:16] + got[3][8:16]
    far_k = fkv[:, :, 0:32, :].reshape(ROWS, HD)
    far_v = fkv[:, :, 32:64, :].reshape(ROWS, HD)
    prob = e_f[...].astype(F32) * (stat[0:1] + stat[1:2])
    ds = low(prob * (nt(far_v, fd) - (stat[2:3] + stat[3:4])))
    fgr[:, :, 0:32, :] = low(nn(ds, fq) * SCALE).reshape(NZ, 2, 32, HD)
    fgr[:, :, 32:64, :] = low(nn(low(prob), fd)).reshape(NZ, 2, 32, HD)
    p6 = [rc(fgr.at[(z + d + 1) % NZ], rz.at[d], 20 + d, zps[d]) for d in range(7)]
    for d in (3, 2, 4, 1, 5, 0, 6):
        p6[d].start()
    fdq = tn(ds, far_k)[0:32] * SCALE

    def near_bwd(h):
        dd = low(nn(a_n[h], do_[:, hc(h)]))
        prob = e_n[h].astype(F32) * (c_n[h, 0:1, :] + c_n[h, 1:2, :])
        ds = low(prob * (nt(near_v(h), dd) - (c_n[h, 2:3, :] + c_n[h, 3:4, :])))
        ng[:, 0:128, hc(h)] = low(nn(ds, q_n[h]) * SCALE).reshape(4, HD, HD)
        ng[:, 128:256, hc(h)] = low(nn(low(prob), dd)).reshape(4, HD, HD)
        dqt[h] = nn(low(tn(near_k(h), ds) * SCALE), a_n[h])

    for h in range(HEADS):
        near_bwd(h)

    back_z = rc(ng.at[0], nrb.at[0], 46, zpart)
    back_x = rc(ng.at[(pos + 3) % 4], nrb.at[1], 47, xpart)
    back_rx = rc(ng.at[0], nrb.at[2], 48, xpart)
    back_rz = rc(ng.at[1], nrb.at[2], 48, zpart)

    @pl.when(z % 2 == 1)
    def _():
        back_x.start()
        back_z.start()

    for cp in p6:
        cp.wait_recv()
    total = fgr[z].astype(F32)
    for d in range(7):
        total = total + rz[d].astype(F32)
    fgr[z] = low(total)
    for hh in range(2):
        for t in range(NY):
            r = slice(8 * t, 8 * t + 8)
            third = jnp.where(xh == hh, fdq[r], 0.0)
            p8s[hh, t] = low(jnp.concatenate(
                [total[hh, r], total[hh, 32 + 8 * t:40 + 8 * t], third, pad8], 0))
    p8 = [rc(p8s.at[yx[n][1], yx[n][0]], p8r.at[xh, y], 29 + n, dev(yx[n][0], z, yx[n][1])) for n in range(7)]
    for cp in p8:
        cp.start()
    p8r[xh, y] = p8s[xh, y]

    def add_block(dst, src):
        dst[...] = low(dst[...].astype(F32) + src[...].astype(F32))

    @pl.when(pos == 1)
    def _():
        back_z.wait_recv()
        add_block(ng.at[0], nrb.at[0])
        back_rx.start()

    @pl.when(pos == 3)
    def _():
        back_x.wait_recv()
        add_block(ng.at[1], nrb.at[1])
        back_rz.start()

    for n in range(2):
        mcs[1, half(n), :] = low(mixed_part(l, 1 - c, n))
        cm1[n].start()
    for n in range(2):
        mkeep[half(n), :] = mixed_part(l, c, n)

    def local_bwd(h):
        for ib in range(2):
            nk = 256 * (ib + 1)
            qs = slice(ib * 256, ib * 256 + 256)
            prob = e_l[h, 0:nk, qs].astype(F32) * c_l[h, 0:1, qs]
            dp = nn(v[0:nk, hc(h)], dot_[hc(h), qs])
            ds = low(prob * (dp - inn[h, 0:1, qs]))
            vt = nn(low(prob), do_[qs, hc(h)])
            kt = nn(ds, q[qs, hc(h)]) * SCALE
            if ib == 0:
                dva[0:nk, hc(h)] = vt
                dka[0:nk, hc(h)] = kt
            else:
                dva[0:256, hc(h)] = dva[0:256, hc(h)] + vt[0:256]
                dka[0:256, hc(h)] = dka[0:256, hc(h)] + kt[0:256]
                dva[256:512, hc(h)] = vt[256:512]
                dka[256:512, hc(h)] = kt[256:512]
            qt = tn(k[0:nk, hc(h)], ds) * SCALE + dqt[h, :, qs]
            dqa[qs, hc(h)] = qt.T

    for h in range(HEADS):
        local_bwd(h)
    for n in range(2):
        cm1[n].wait()
        cmx[n].wait()
        mixed[half(n), :] = low(mkeep[half(n), :] + mcr[1, half(n), :].astype(F32) + mxr[half(n), :].astype(F32))

    @pl.when(pos == 0)
    def _():
        back_z.wait_recv()
        add_block(ng.at[0], nrb.at[0])
        back_rx.wait_recv()
        add_block(ng.at[0], nrb.at[2])

    @pl.when(pos == 1)
    def _():
        back_rz.wait_recv()
        add_block(ng.at[1], nrb.at[2])

    @pl.when(pos == 2)
    def _():
        back_x.wait_recv()
        add_block(ng.at[2], nrb.at[1])

    for cp in p8:
        cp.wait()
    jt = iota((ROWS, HD), 0)
    at = iota((ROWS, HD), 1)
    jf = iota((ROWS, 16), 0)
    af = iota((ROWS, 16), 1)
    for h in range(HEADS):
        back_n = jnp.where(jt == 4 * at + offs[0, h], 1.0, 0.0).astype(BF)
        back_f = jnp.where((jf == 64 * af + offs[1, h]) & (af < 8), 1.0, 0.0).astype(BF)
        x = p8r[0, h].astype(F32) + p8r[1, h].astype(F32)
        wide = jnp.concatenate([x[0:8], x[8:16], x[16:24]], 1)
        far = nn(back_f, low(jnp.concatenate([wide, jnp.zeros((8, 3 * HD), F32)], 0)))
        dk[:, hc(h)] = low(dka[:, hc(h)] + nn(back_n, ng[pos, 0:128, hc(h)]) + far[:, 0:HD])
        dv[:, hc(h)] = low(dva[:, hc(h)] + nn(back_n, ng[pos, 128:256, hc(h)]) + far[:, HD:2 * HD])
        dq[:, hc(h)] = low(dqa[:, hc(h)] + far[:, 2 * HD:])

    for cp in p3 + p6:
        cp.wait_send()

    @pl.when(xh == 0)
    def _():
        for cp in near_x:
            cp.wait_send()

    @pl.when(z_even)
    def _():
        for cp in near_z:
            cp.wait_send()

    @pl.when(pos == 1)
    def _():
        for cp in relay_z:
            cp.wait_send()
        back_rx.wait_send()

    @pl.when(pos == 3)
    def _():
        for cp in relay_x:
            cp.wait_send()
        back_rz.wait_send()

    @pl.when(z % 2 == 1)
    def _():
        back_x.wait_send()
        back_z.wait_send()


def hand_on(a, b, c, d, a2, b2, c2, d2, hold, in_sem, out_sem):
    pairs = [(a, a2), (b, b2), (c, c2), (d, d2)]
    ins = [pltpu.make_async_copy(x, hold.at[j], in_sem.at[j]) for j, (x, _) in enumerate(pairs)]
    outs = [pltpu.make_async_copy(hold.at[j], x, out_sem.at[j]) for j, (_, x) in enumerate(pairs)]
    for cp in ins:
        cp.start()
    for i, o in zip(ins, outs):
        i.wait()
        o.start()
    for cp in outs:
        cp.wait()


def local(queries, key_rows, value_rows, out_weight, grad_out, offsets):
    vm = pl.BlockSpec(memory_space=pltpu.VMEM)
    hbm = pl.BlockSpec(memory_space=pl.ANY)
    shape = jax.ShapeDtypeStruct((ROWS, ROWS), BF)
    V = pltpu.VMEM
    dma = pltpu.SemaphoreType.DMA
    wide = (ROWS, ROWS)
    outs = pl.pallas_call(
        kernel,
        out_shape=(shape,) * 4,
        in_specs=[pl.BlockSpec(memory_space=pltpu.SMEM)] + [hbm] * 5,
        out_specs=(vm,) * 4,
        scratch_shapes=[
            V(wide, BF), V(wide, BF), V(wide, BF), V((ROWS, 4 * ROWS), BF), V(wide, BF),
            V((3, ROWS, ROWS), BF), V(wide, F32), V(wide, BF), V(wide, BF),
            V((4, 256, ROWS), BF),
            V((HEADS, ROWS, ROWS), BF), V((HEADS, ROWS, HD), BF), V((ROWS, HD), BF),
            V((HEADS, HD, ROWS), F32), V((HEADS, 144, HD), BF),
            V((HEADS, 8, ROWS), F32), V((HEADS, 8, HD), F32),
            V((HEADS, HD, HD), BF),
            V((HEADS, HD, ROWS), BF), V((HEADS, HD, ROWS), BF), V((HEADS, 16, ROWS), BF),
            V(wide, BF),
            V((HEADS, 8, ROWS), F32), V((HEADS, 16, HD), F32), V((HEADS, 8, ROWS), F32),
            V((HEADS, HD, ROWS), F32), V(wide, F32), V(wide, F32), V(wide, F32),
            V((NY, 32, HD), BF), V((2, NY, 32, HD), BF), V((NZ, 2, 64, HD), BF), V((NY, 144, HD), BF),
            V((NY, 16, HD), BF), V((NY, 16, HD), BF), V((NZ, 2, 64, HD), BF), V((NZ - 1, 2, 64, HD), BF),
            V((2, NY, 32, HD), BF), V((2, NY, 32, HD), BF),
            V((4, 256, ROWS), BF), V((3, 256, ROWS), BF),
            V((2, ROWS, ROWS), BF), V((2, ROWS, ROWS), BF), V(wide, F32),
            V(wide, BF), V(wide, BF),
            dma((5,)), dma((60,)), dma((60,)),
        ],
        compiler_params=pltpu.CompilerParams(
            collective_id=0, has_side_effects=True, vmem_limit_bytes=56 << 20),
        cost_estimate=pl.CostEstimate(flops=4_400_000_000, bytes_accessed=8 << 20, transcendentals=1_400_000),
        name="dilated",
    )(offsets, queries, key_rows, value_rows, out_weight, grad_out)
    return pl.pallas_call(
        hand_on,
        out_shape=(shape,) * 4,
        in_specs=[hbm] * 4,
        out_specs=(hbm,) * 4,
        scratch_shapes=[V((4, ROWS, ROWS), BF), dma((4,)), dma((4,))],
        name="hand_on",
    )(*outs)


def solution(mesh):
    return jax.shard_map(
        local,
        mesh=mesh,
        in_specs=(
            P("seq", "mp"),
            P("seq", "mp"),
            P("seq", "mp"),
            P("mp", None),
            P("seq", "mp"),
            P(None, "mp"),
        ),
        out_specs=(P("seq", "mp"), P("seq", "mp"), P("seq", "mp"), P("seq", "mp")),
        check_vma=False,
    )
```

time: 91.9 us -> 67.4 us (0.73)
  the two profiles are of different devices: /device:TPU:2 before, /device:TPU:28 now
where the time goes in v2:
time: 67.4 us; the launch traced here: 67.3 us
  Pallas kernels  66.5 us (99%)
  between operations  0.8 us (1%)
    pallas_call x1, Pallas kernels, local(): pl.pallas_call(kernel, out_shape=(shape,) * 4, in_specs=[pl.BlockSpec(mem...  64.1 us
    pallas_call x1, Pallas kernels, local(): pl.pallas_call(hand_on, out_shape=(shape,) * 4, in_specs=[hbm] * 4, out_s...  2.42 us

profile of v2, /device:TPU:28, one launch (start us, length us, event | category | flops | bytes accessed | tf_op | source)
XLA Modules:
  0.0 67.3 jit_solution(8016253849065615321)
XLA Ops:
  0.6 64.1 %dilated.1 = (bf16[512,512]{1,0:T(8,128)(2,1)}, bf16[512,512]{1,0:T(8,128)(2,1)}, bf16[512,512]{1,0:T(8,128)(2,1)}, bf16[512,512]{1,0:T(8,128)(2,1)}) custom-call(s32[2,4]{1,0:T(2,128)} %offs.1, bf16[512,512]{1,0:T(8,128)(2,1)} %qh.1, bf16[512,512]{1,0:T(8,128)(2,1)} %kh.1, bf16[512,512]{1,0:T(8,128)(2,1)} %vh.1, bf16[512,2048]{1,0:T(8,128)(2,1)} %wh.1, ...), custom_call_target="tpu_custom_call" | custom-call | flops 4400000000 | bytes 8388608 | tf_op jit(solution)/shard_map/dilated/pallas_call | solution.py:508
  64.7 2.4 %hand_on.1 = (bf16[512,512]{1,0:T(8,128)(2,1)}, bf16[512,512]{1,0:T(8,128)(2,1)}, bf16[512,512]{1,0:T(8,128)(2,1)}, bf16[512,512]{1,0:T(8,128)(2,1)}) custom-call(bf16[512,512]{1,0:T(8,128)(2,1)} %get-tuple-element.8.a, bf16[512,512]{1,0:T(8,128)(2,1)} %get-tuple-element.9.b, bf16[512,512]{1,0:T(8,128)(2,1)} %get-tuple-element.10.c, ...), custom_call_target="tpu_custom_call" | custom-call | tf_op jit(solution)/shard_map/hand_on/pallas_call | solution.py:538

commit v3 on v2

--- a/solution.py
+++ b/solution.py
@@ -43,12 +43,12 @@
     return hi, x - hi
 
 
-def kernel(offs, qh, kh, vh, wh, gh, mixed, dq, dk, dv,
+def kernel(offs, qh, kh, vh, wh, gh, mixed_h, dq_h, dk_h, dv_h, mixed, dq, dk, dv,
            q, k, v, w, g, gbuf, gacc, dot_, do_, nkv, e_l, e_n, e_f, o_l, o_n,
            st_l, st_n, q_n, a_n, a_f, f16, att, c_l, c_n, inn, dqt, dqa, dka, dva,
            p1s, p1r, fkv, fo, p5s, p5r, fgr, rz, p8s, p8r,
            ng, nrb, mcs, mcr, mkeep, mxs, mxr,
-           ins, ss, rs):
+           back_n, back_f, ins, outs, ss, rs):
     s = lax.axis_index("seq")
     m = lax.axis_index("mp")
     y, z, xh = s // 16, (s // 2) % NZ, s % 2
@@ -98,22 +98,20 @@
         rows = [nn(f16[h], x[:, hc(h)])[:8] for x in (k, v, q)]
         p1s[h] = low(jnp.concatenate(rows + [pad8], 0))
     for h in range(HEADS):
-        nkv[pos, 0:128, hc(h)] = low(nn(a_n[h], k[:, hc(h)]))
-        nkv[pos, 128:256, hc(h)] = low(nn(a_n[h], v[:, hc(h)]))
+        nkv[pos, h, 0:128, :] = low(nn(a_n[h], k[:, hc(h)]))
+        nkv[pos, h, 128:256, :] = low(nn(a_n[h], v[:, hc(h)]))
     for t in range(1, 4):
-        @pl.when(t > pos)
+        @pl.when((t > pos + 1) | ((t == pos + 1) & (pos > 0)))
         def _():
-            nkv[t] = jnp.zeros((256, ROWS), BF)
+            nkv[t] = jnp.zeros((HEADS, 256, HD), BF)
 
     def near_send(base, slot, to):
-        return [rc(nkv.at[slot, pl.ds(128 * n, 128)], nkv.at[slot, pl.ds(128 * n, 128)], base + n, to)
-                for n in range(2)]
+        return [rc(nkv.at[slot, h], nkv.at[slot, h], base + h, to) for h in range(HEADS)]
 
     z_even = z % 2 == 0
     near_z = near_send(40, pos, zpart)
-    near_x = near_send(42, pos, xpart)
-    relay_z = near_send(44, 0, zpart)
-    relay_x = near_send(44, 1, xpart)
+    near_x = near_send(44, pos, xpart)
+    relay = near_send(48, (pos + 1) % 2, zpart)
 
     def local_fwd(h):
         for ib in range(2):
@@ -141,7 +139,7 @@
         cp.start()
     p1r[xh, y] = p1s[y]
 
-    @pl.when(xh == 0)
+    @pl.when(pos != 3)
     def _():
         for cp in near_x:
             cp.start()
@@ -151,14 +149,14 @@
         for cp in near_z:
             cp.start()
 
-    def halves(src, dst, base, to):
-        return [rc(src.at[pl.ds(256 * n, 256)], dst.at[pl.ds(256 * n, 256)], base + n, to) for n in range(2)]
-
-    cg_x = halves(g, gbuf.at[1], 50, across)
+    def pieces(src, dst, base, to, count):
+        size = ROWS // count
+        return [rc(src.at[pl.ds(size * n, size)], dst.at[pl.ds(size * n, size)], base + n, to)
+                for n in range(count)]
+
+    cg_x = pieces(g, gbuf.at[1], 52, across, 4)
     cg_core = rc(g, gbuf.at[0], 28, core)
-    cg_f = halves(gbuf.at[1], gbuf.at[2], 52, core)
-    for cp in cg_x:
-        cp.start()
+    cg_f = pieces(gbuf.at[1], gbuf.at[2], 56, core, 4)
     cg_core.start()
     local_fwd(2)
     local_fwd(3)
@@ -170,33 +168,32 @@
     p3 = [rc(fkv.at[z], fkv.at[z], 7 + d, zps[d]) for d in range(7)]
     for d in (3, 2, 4, 1, 5, 0, 6):
         p3[d].start()
+    for cp in cg_x:
+        cp.start()
     got = [p1r[xh, t].astype(F32) for t in range(NY)]
     fq = low(jnp.concatenate([x[16:24] for x in got] + [jnp.zeros((96, HD), F32)], 0))
 
-    def grad_part(slot):
+    def grad_part(slot, half):
         src = [(l, c), (l, 1 - c), (1 - l, c), (1 - l, 1 - c)][slot]
         cols = pl.ds(pl.multiple_of((src[0] * 2 + src[1]) * ROWS, ROWS), ROWS)
-        part = nt(w[:, cols], g[...] if slot == 0 else gbuf[slot - 1])
+        r = slice(256 * half, 256 * half + 256)
+        part = nt(w[:, cols], g[r, :] if slot == 0 else gbuf[slot - 1, r, :])
         if slot:
-            part = part + gacc[...]
-        gacc[...] = part
+            part = part + gacc[:, r]
+        gacc[:, r] = part
 
     loads[4].wait()
-    grad_part(0)
+    for n in range(2):
+        grad_part(0, n)
     cg_core.wait()
-    grad_part(1)
-
-    @pl.when(pos == 1)
-    def _():
-        for n in range(2):
-            near_x[n].wait_recv()
-            relay_z[n].start()
-
-    @pl.when(pos == 3)
-    def _():
-        for n in range(2):
-            near_z[n].wait_recv()
-            relay_x[n].start()
+    for n in range(2):
+        grad_part(1, n)
+
+    @pl.when(z_even)
+    def _():
+        for h in range(HEADS):
+            near_x[h].wait_recv()
+            relay[h].start()
 
     def scores(kk, qq, vv, seen):
         st = nt(kk, qq) * SCALE
@@ -215,10 +212,16 @@
     far_seen = key_index <= query_index
 
     def near_k(h):
-        return nkv[:, 0:128, hc(h)].reshape(ROWS, HD)
+        return nkv[:, h, 0:128, :].reshape(ROWS, HD)
 
     def near_v(h):
-        return nkv[:, 128:256, hc(h)].reshape(ROWS, HD)
+        return nkv[:, h, 128:256, :].reshape(ROWS, HD)
+
+    jt = iota((ROWS, HD), 0)
+    at = iota((ROWS, HD), 1)
+    for h in range(HEADS):
+        back_n[h] = jnp.where(jt == 4 * at + offs[0, h], 1.0, 0.0).astype(BF)
+        back_f[h] = jnp.where((jt == 64 * at + offs[1, h]) & (at < 8), 1.0, 0.0).astype(BF)[:, 0:16]
 
     for cp in p3:
         cp.wait_recv()
@@ -231,29 +234,16 @@
     for cp in p4:
         cp.start()
 
-    for n in range(2):
-        cg_x[n].wait()
-        cg_f[n].start()
-    grad_part(2)
-    for n in range(2):
-        cg_f[n].wait()
-    grad_part(3)
-    dot_[...] = low(gacc[...])
-    do_[...] = low(gacc[...].T)
-
-    @pl.when(pos == 2)
-    def _():
-        for n in range(2):
-            near_z[n].wait_recv()
-            relay_x[n].wait_recv()
-
-    @pl.when(pos == 3)
-    def _():
-        for n in range(2):
-            near_x[n].wait_recv()
-            relay_z[n].wait_recv()
-
-    for h in range(HEADS):
+    for h in range(HEADS):
+        @pl.when(z % 2 == 1)
+        def _():
+            near_z[h].wait_recv()
+            relay[h].wait_recv()
+
+        @pl.when(pos == 3)
+        def _():
+            near_x[h].wait_recv()
+
         qq = low(nn(a_n[h], q[:, hc(h)]))
         q_n[h] = qq
         el, block = scores(near_k(h), qq, near_v(h), near_seen)
@@ -284,22 +274,21 @@
         inv = 1.0 / total
         out = low((o_l[h] * wl + on * wn + of * wf) * inv)
         att[hc(h), :] = out
-        inner = jnp.sum(dot_[hc(h), :].astype(F32) * out.astype(F32), 0, keepdims=True)
         c_l[h, 0:1, :] = wl * inv
+        c_l[h, 1:2, :] = wn * inv
+        c_l[h, 2:3, :] = wf * inv
+
+    def row_stats(h):
+        inner = jnp.sum(dot_[hc(h), :].astype(F32) * att[hc(h), :].astype(F32), 0, keepdims=True)
         inn[h, 0:1, :] = inner
-        far = picked(wf * inv, inner, a_f[h])
+        far = picked(c_l[h, 2:3, :], inner, a_f[h])
         p5s[h] = low(jnp.concatenate([nn(f16[h], do_[:, hc(h)])[:8], far[:8]], 0))
-        c_n[h] = picked(wn * inv, inner, a_n[h])
+        c_n[h] = picked(c_l[h, 1:2, :], inner, a_n[h])
 
     for cp in p4:
         cp.wait()
     for h in range(HEADS):
         combine(h)
-    p5 = [rc(p5s.at[ys[d]], p5r.at[y], 17 + d, yps[d]) for d in range(3)]
-    for cp in p5:
-        cp.start()
-    p5r[y] = p5s[y]
-
     def mixed_part(ll, cc, n):
         cols = pl.ds(pl.multiple_of((ll * 2 + cc) * ROWS, ROWS), ROWS)
         return tn(att[:, 256 * n:256 * n + 256], w[:, cols])
@@ -307,9 +296,15 @@
     def half(n):
         return pl.ds(256 * n, 256)
 
-    cm0 = halves(mcs.at[0], mcr.at[0], 54, core)
-    cm1 = halves(mcs.at[1], mcr.at[1], 56, core)
-    cmx = halves(mxs, mxr, 58, across)
+    cm0 = pieces(mcs.at[0], mcr.at[0], 60, core, 2)
+    cm1 = pieces(mcs.at[1], mcr.at[1], 62, core, 2)
+    cmx = [rc(mxs.at[pl.ds(64 * n, 64)], mxr.at[pl.ds(64 * n, 64)], 64 + n, across) for n in range(8)]
+
+    def send_mixed(n):
+        if n >= 2:
+            cmx[n - 2].wait_send()
+        cmx[n].start()
+
     for n in range(2):
         mcs[0, half(n), :] = low(mixed_part(1 - l, 1 - c, n))
         cm0[n].start()
@@ -317,7 +312,49 @@
         part = mixed_part(1 - l, c, n)
         cm0[n].wait()
         mxs[half(n), :] = low(part + mcr[0, half(n), :].astype(F32))
-        cmx[n].start()
+        send_mixed(n)
+
+    for n in range(2):
+        for i in (2 * n, 2 * n + 1):
+            cg_x[i].wait_recv()
+            cg_f[i].start()
+        grad_part(2, n)
+    for n in range(2):
+        cg_f[2 * n].wait_recv()
+        cg_f[2 * n + 1].wait_recv()
+        grad_part(3, n)
+        r = slice(256 * n, 256 * n + 256)
+        dot_[:, r] = low(gacc[:, r])
+        do_[r, :] = dot_[:, r].T
+    for h in range(HEADS):
+        row_stats(h)
+    p5 = [rc(p5s.at[ys[d]], p5r.at[y], 17 + d, yps[d]) for d in range(3)]
+    for cp in p5:
+        cp.start()
+    p5r[y] = p5s[y]
+
+    def near_bwd(h):
+        dd = low(nn(a_n[h], do_[:, hc(h)]))
+        prob = e_n[h].astype(F32) * (c_n[h, 0:1, :] + c_n[h, 1:2, :])
+        ds = low(prob * (nt(near_v(h), dd) - (c_n[h, 2:3, :] + c_n[h, 3:4, :])))
+        ng[:, h, 0:128, :] = low(nn(ds, q_n[h]) * SCALE).reshape(4, HD, HD)
+        ng[:, h, 128:256, :] = low(nn(low(prob), dd)).reshape(4, HD, HD)
+        dqt[h] = nn(low(tn(near_k(h), ds) * SCALE), a_n[h])
+
+    def back_copy(slot, into, base, to):
+        return [rc(ng.at[slot, h], nrb.at[into, h], base + h, to) for h in range(HEADS)]
+
+    back_z = back_copy(0, 0, 72, zpart)
+    back_x = back_copy((pos + 3) % 4, 1, 76, xpart)
+    back_rx = back_copy(0, 2, 80, xpart)
+    back_rz = back_copy(1, 2, 80, zpart)
+    for h in range(HEADS):
+        near_bwd(h)
+
+        @pl.when(z % 2 == 1)
+        def _():
+            back_z[h].start()
+            back_x[h].start()
 
     for cp in p5:
         cp.wait()
@@ -334,65 +371,6 @@
     for d in (3, 2, 4, 1, 5, 0, 6):
         p6[d].start()
     fdq = tn(ds, far_k)[0:32] * SCALE
-
-    def near_bwd(h):
-        dd = low(nn(a_n[h], do_[:, hc(h)]))
-        prob = e_n[h].astype(F32) * (c_n[h, 0:1, :] + c_n[h, 1:2, :])
-        ds = low(prob * (nt(near_v(h), dd) - (c_n[h, 2:3, :] + c_n[h, 3:4, :])))
-        ng[:, 0:128, hc(h)] = low(nn(ds, q_n[h]) * SCALE).reshape(4, HD, HD)
-        ng[:, 128:256, hc(h)] = low(nn(low(prob), dd)).reshape(4, HD, HD)
-        dqt[h] = nn(low(tn(near_k(h), ds) * SCALE), a_n[h])
-
-    for h in range(HEADS):
-        near_bwd(h)
-
-    back_z = rc(ng.at[0], nrb.at[0], 46, zpart)
-    back_x = rc(ng.at[(pos + 3) % 4], nrb.at[1], 47, xpart)
-    back_rx = rc(ng.at[0], nrb.at[2], 48, xpart)
-    back_rz = rc(ng.at[1], nrb.at[2], 48, zpart)
-
-    @pl.when(z % 2 == 1)
-    def _():
-        back_x.start()
-        back_z.start()
-
-    for cp in p6:
-        cp.wait_recv()
-    total = fgr[z].astype(F32)
-    for d in range(7):
-        total = total + rz[d].astype(F32)
-    fgr[z] = low(total)
-    for hh in range(2):
-        for t in range(NY):
-            r = slice(8 * t, 8 * t + 8)
-            third = jnp.where(xh == hh, fdq[r], 0.0)
-            p8s[hh, t] = low(jnp.concatenate(
-                [total[hh, r], total[hh, 32 + 8 * t:40 + 8 * t], third, pad8], 0))
-    p8 = [rc(p8s.at[yx[n][1], yx[n][0]], p8r.at[xh, y], 29 + n, dev(yx[n][0], z, yx[n][1])) for n in range(7)]
-    for cp in p8:
-        cp.start()
-    p8r[xh, y] = p8s[xh, y]
-
-    def add_block(dst, src):
-        dst[...] = low(dst[...].astype(F32) + src[...].astype(F32))
-
-    @pl.when(pos == 1)
-    def _():
-        back_z.wait_recv()
-        add_block(ng.at[0], nrb.at[0])
-        back_rx.start()
-
-    @pl.when(pos == 3)
-    def _():
-        back_x.wait_recv()
-        add_block(ng.at[1], nrb.at[1])
-        back_rz.start()
-
-    for n in range(2):
-        mcs[1, half(n), :] = low(mixed_part(l, 1 - c, n))
-        cm1[n].start()
-    for n in range(2):
-        mkeep[half(n), :] = mixed_part(l, c, n)
 
     def local_bwd(h):
         for ib in range(2):
@@ -414,75 +392,132 @@
             qt = tn(k[0:nk, hc(h)], ds) * SCALE + dqt[h, :, qs]
             dqa[qs, hc(h)] = qt.T
 
-    for h in range(HEADS):
-        local_bwd(h)
+    def add_block(dst, src):
+        dst[...] = low(dst[...].astype(F32) + src[...].astype(F32))
+
+    def relay_back(heads):
+        @pl.when(pos == 1)
+        def _():
+            for h in heads:
+                back_z[h].wait_recv()
+                add_block(ng.at[0, h], nrb.at[0, h])
+                back_rx[h].start()
+
+        @pl.when(pos == 3)
+        def _():
+            for h in heads:
+                back_x[h].wait_recv()
+                add_block(ng.at[1, h], nrb.at[1, h])
+                back_rz[h].start()
+
+    relay_back((0, 1))
+    send_mixed(2)
+    local_bwd(0)
+    relay_back((2, 3))
+    send_mixed(3)
+    local_bwd(1)
+    send_mixed(4)
+    local_bwd(2)
+    send_mixed(5)
+    for cp in p6:
+        cp.wait_recv()
+    total = fgr[z].astype(F32)
+    for d in range(7):
+        total = total + rz[d].astype(F32)
+    fgr[z] = low(total)
+    for hh in range(2):
+        for t in range(NY):
+            r = slice(8 * t, 8 * t + 8)
+            third = jnp.where(xh == hh, fdq[r], 0.0)
+            p8s[hh, t] = low(jnp.concatenate(
+                [total[hh, r], total[hh, 32 + 8 * t:40 + 8 * t], third, pad8], 0))
+    p8 = [rc(p8s.at[yx[n][1], yx[n][0]], p8r.at[xh, y], 29 + n, dev(yx[n][0], z, yx[n][1])) for n in range(7)]
+    for cp in p8:
+        cp.start()
+    p8r[xh, y] = p8s[xh, y]
+
+    local_bwd(3)
+    send_mixed(6)
+    for n in range(2):
+        mcs[1, half(n), :] = low(mixed_part(l, 1 - c, n))
+        cm1[n].start()
+    send_mixed(7)
+    for n in range(2):
+        mkeep[half(n), :] = mixed_part(l, c, n)
+
+    cmx[6].wait_send()
+    cmx[7].wait_send()
     for n in range(2):
         cm1[n].wait()
-        cmx[n].wait()
+        for i in range(4):
+            cmx[4 * n + i].wait_recv()
         mixed[half(n), :] = low(mkeep[half(n), :] + mcr[1, half(n), :].astype(F32) + mxr[half(n), :].astype(F32))
 
+    out_mixed = pltpu.make_async_copy(mixed, mixed_h, outs.at[0])
+    out_mixed.start()
+
+    def take(copies, slot, into):
+        for cp in copies:
+            cp.wait_recv()
+        add_block(ng.at[slot], nrb.at[into])
+
     @pl.when(pos == 0)
     def _():
-        back_z.wait_recv()
-        add_block(ng.at[0], nrb.at[0])
-        back_rx.wait_recv()
-        add_block(ng.at[0], nrb.at[2])
+        take(back_z, 0, 0)
+        take(back_rx, 0, 2)
 
     @pl.when(pos == 1)
     def _():
-        back_rz.wait_recv()
-        add_block(ng.at[1], nrb.at[2])
+        take(back_rz, 1, 2)
 
     @pl.when(pos == 2)
     def _():
-        back_x.wait_recv()
-        add_block(ng.at[2], nrb.at[1])
+        take(back_x, 2, 1)
 
     for cp in p8:
         cp.wait()
-    jt = iota((ROWS, HD), 0)
-    at = iota((ROWS, HD), 1)
-    jf = iota((ROWS, 16), 0)
-    af = iota((ROWS, 16), 1)
-    for h in range(HEADS):
-        back_n = jnp.where(jt == 4 * at + offs[0, h], 1.0, 0.0).astype(BF)
-        back_f = jnp.where((jf == 64 * af + offs[1, h]) & (af < 8), 1.0, 0.0).astype(BF)
+    out_rest = []
+    for h in range(HEADS):
         x = p8r[0, h].astype(F32) + p8r[1, h].astype(F32)
         wide = jnp.concatenate([x[0:8], x[8:16], x[16:24]], 1)
-        far = nn(back_f, low(jnp.concatenate([wide, jnp.zeros((8, 3 * HD), F32)], 0)))
-        dk[:, hc(h)] = low(dka[:, hc(h)] + nn(back_n, ng[pos, 0:128, hc(h)]) + far[:, 0:HD])
-        dv[:, hc(h)] = low(dva[:, hc(h)] + nn(back_n, ng[pos, 128:256, hc(h)]) + far[:, HD:2 * HD])
+        far = nn(back_f[h], low(jnp.concatenate([wide, jnp.zeros((8, 3 * HD), F32)], 0)))
+        dk[:, hc(h)] = low(dka[:, hc(h)] + nn(back_n[h], ng[pos, h, 0:128, :]) + far[:, 0:HD])
+        dv[:, hc(h)] = low(dva[:, hc(h)] + nn(back_n[h], ng[pos, h, 128:256, :]) + far[:, HD:2 * HD])
         dq[:, hc(h)] = low(dqa[:, hc(h)] + far[:, 2 * HD:])
-
-    for cp in p3 + p6:
+        for n, (a, b) in enumerate([(dk, dk_h), (dv, dv_h), (dq, dq_h)]):
+            cp = pltpu.make_async_copy(a.at[:, hc(h)], b.at[:, hc(h)], outs.at[1 + 3 * h + n])
+            cp.start()
+            out_rest.append(cp)
+
+    for cp in p3 + p6 + cg_x + cg_f:
         cp.wait_send()
 
-    @pl.when(xh == 0)
+    @pl.when(pos != 3)
     def _():
         for cp in near_x:
             cp.wait_send()
 
     @pl.when(z_even)
     def _():
-        for cp in near_z:
+        for cp in near_z + relay:
             cp.wait_send()
 
     @pl.when(pos == 1)
     def _():
-        for cp in relay_z:
+        for cp in back_rx:
             cp.wait_send()
-        back_rx.wait_send()
 
     @pl.when(pos == 3)
     def _():
-        for cp in relay_x:
+        for cp in back_rz:
             cp.wait_send()
-        back_rz.wait_send()
 
     @pl.when(z % 2 == 1)
     def _():
-        back_x.wait_send()
-        back_z.wait_send()
+        for cp in back_x + back_z:
+            cp.wait_send()
+    for cp in [out_mixed] + out_rest:
+        cp.wait()
 
 
 def hand_on(a, b, c, d, a2, b2, c2, d2, hold, in_sem, out_sem):
@@ -499,7 +534,6 @@
 
 
 def local(queries, key_rows, value_rows, out_weight, grad_out, offsets):
-    vm = pl.BlockSpec(memory_space=pltpu.VMEM)
     hbm = pl.BlockSpec(memory_space=pl.ANY)
     shape = jax.ShapeDtypeStruct((ROWS, ROWS), BF)
     V = pltpu.VMEM
@@ -509,11 +543,12 @@
         kernel,
         out_shape=(shape,) * 4,
         in_specs=[pl.BlockSpec(memory_space=pltpu.SMEM)] + [hbm] * 5,
-        out_specs=(vm,) * 4,
+        out_specs=(hbm,) * 4,
         scratch_shapes=[
+            V(wide, BF), V(wide, BF), V(wide, BF), V(wide, BF),
             V(wide, BF), V(wide, BF), V(wide, BF), V((ROWS, 4 * ROWS), BF), V(wide, BF),
             V((3, ROWS, ROWS), BF), V(wide, F32), V(wide, BF), V(wide, BF),
-            V((4, 256, ROWS), BF),
+            V((4, HEADS, 256, HD), BF),
             V((HEADS, ROWS, ROWS), BF), V((HEADS, ROWS, HD), BF), V((ROWS, HD), BF),
             V((HEADS, HD, ROWS), F32), V((HEADS, 144, HD), BF),
             V((HEADS, 8, ROWS), F32), V((HEADS, 8, HD), F32),
@@ -525,10 +560,11 @@
             V((NY, 32, HD), BF), V((2, NY, 32, HD), BF), V((NZ, 2, 64, HD), BF), V((NY, 144, HD), BF),
             V((NY, 16, HD), BF), V((NY, 16, HD), BF), V((NZ, 2, 64, HD), BF), V((NZ - 1, 2, 64, HD), BF),
             V((2, NY, 32, HD), BF), V((2, NY, 32, HD), BF),
-            V((4, 256, ROWS), BF), V((3, 256, ROWS), BF),
+            V((4, HEADS, 256, HD), BF), V((3, HEADS, 256, HD), BF),
             V((2, ROWS, ROWS), BF), V((2, ROWS, ROWS), BF), V(wide, F32),
             V(wide, BF), V(wide, BF),
-            dma((5,)), dma((60,)), dma((60,)),
+            V((HEADS, ROWS, HD), BF), V((HEADS, ROWS, 16), BF),
+            dma((5,)), dma((13,)), dma((84,)), dma((84,)),
         ],
         compiler_params=pltpu.CompilerParams(
             collective_id=0, has_side_effects=True, vmem_limit_bytes=56 << 20),

time: 67.4 us -> 63.1 us (0.936)
  the two profiles are of different devices: /device:TPU:28 before, /device:TPU:1 now
where the time goes in v3:
time: 63.1 us; the launch traced here: 61.9 us
  Pallas kernels  61.1 us (97%)
  between operations  0.8 us (1%)
    pallas_call x1, Pallas kernels, local(): pl.pallas_call(kernel, out_shape=(shape,) * 4, in_specs=[pl.BlockSpec(mem...  58.7 us
    pallas_call x1, Pallas kernels, local(): pl.pallas_call(hand_on, out_shape=(shape,) * 4, in_specs=[hbm] * 4, out_s...  2.42 us

profile of v3, /device:TPU:1, one launch (start us, length us, event | category | flops | bytes accessed | tf_op | source)
XLA Modules:
  0.0 61.9 jit_solution(12670373668128759876)
XLA Ops:
  0.6 58.7 %dilated.1 = (bf16[512,512]{1,0:T(8,128)(2,1)}, bf16[512,512]{1,0:T(8,128)(2,1)}, bf16[512,512]{1,0:T(8,128)(2,1)}, bf16[512,512]{1,0:T(8,128)(2,1)}) custom-call(s32[2,4]{1,0:T(2,128)} %offs.1, bf16[512,512]{1,0:T(8,128)(2,1)} %qh.1, bf16[512,512]{1,0:T(8,128)(2,1)} %kh.1, bf16[512,512]{1,0:T(8,128)(2,1)} %vh.1, bf16[512,2048]{1,0:T(8,128)(2,1)} %wh.1, ...), custom_call_target="tpu_custom_call" | custom-call | flops 4400000000 | bytes 8388608 | tf_op jit(solution)/shard_map/dilated/pallas_call | solution.py:542
  59.3 2.4 %hand_on.1 = (bf16[512,512]{1,0:T(8,128)(2,1)}, bf16[512,512]{1,0:T(8,128)(2,1)}, bf16[512,512]{1,0:T(8,128)(2,1)}, bf16[512,512]{1,0:T(8,128)(2,1)}) custom-call(bf16[512,512]{1,0:T(8,128)(2,1)} %get-tuple-element.8.a, bf16[512,512]{1,0:T(8,128)(2,1)} %get-tuple-element.9.b, bf16[512,512]{1,0:T(8,128)(2,1)} %get-tuple-element.10.c, ...), custom_call_target="tpu_custom_call" | custom-call | tf_op jit(solution)/shard_map/hand_on/pallas_call | solution.py:574

commit v4 on v3

--- a/solution.py
+++ b/solution.py
@@ -301,8 +301,8 @@
     cmx = [rc(mxs.at[pl.ds(64 * n, 64)], mxr.at[pl.ds(64 * n, 64)], 64 + n, across) for n in range(8)]
 
     def send_mixed(n):
-        if n >= 2:
-            cmx[n - 2].wait_send()
+        if n >= 4:
+            cmx[n - 4].wait_send()
         cmx[n].start()
 
     for n in range(2):
@@ -312,7 +312,8 @@
         part = mixed_part(1 - l, c, n)
         cm0[n].wait()
         mxs[half(n), :] = low(part + mcr[0, half(n), :].astype(F32))
-        send_mixed(n)
+        send_mixed(2 * n)
+        send_mixed(2 * n + 1)
 
     for n in range(2):
         for i in (2 * n, 2 * n + 1):
@@ -411,14 +412,12 @@
                 back_rz[h].start()
 
     relay_back((0, 1))
-    send_mixed(2)
     local_bwd(0)
     relay_back((2, 3))
-    send_mixed(3)
+    send_mixed(4)
     local_bwd(1)
-    send_mixed(4)
+    send_mixed(5)
     local_bwd(2)
-    send_mixed(5)
     for cp in p6:
         cp.wait_recv()
     total = fgr[z].astype(F32)
@@ -445,8 +444,8 @@
     for n in range(2):
         mkeep[half(n), :] = mixed_part(l, c, n)
 
-    cmx[6].wait_send()
-    cmx[7].wait_send()
+    for n in range(4, 8):
+        cmx[n].wait_send()
     for n in range(2):
         cm1[n].wait()
         for i in range(4):

time: 63.1 us -> 61 us (0.967); the launches traced: 61.9 us -> 60.8 us
  Pallas kernels: 61.1 us -> 60 us
    pallas_call x1, Pallas kernels: 58.7 us -> 57.6 us  [local(): pl.pallas_call(kernel, out_shape=(shape,) * 4, in_specs=[pl.BlockSpec(mem...]
where the time goes in v4:
time: 61 us; the launch traced here: 60.8 us
  Pallas kernels  60 us (98%)
  between operations  0.8 us (1%)
    pallas_call x1, Pallas kernels, local(): pl.pallas_call(kernel, out_shape=(shape,) * 4, in_specs=[pl.BlockSpec(mem...  57.6 us
    pallas_call x1, Pallas kernels, local(): pl.pallas_call(hand_on, out_shape=(shape,) * 4, in_specs=[hbm] * 4, out_s...  2.42 us

profile of v4, /device:TPU:1, one launch (start us, length us, event | category | flops | bytes accessed | tf_op | source)
XLA Modules:
  0.0 60.8 jit_solution(4995153715370383817)
XLA Ops:
  0.6 57.6 %dilated.1 = (bf16[512,512]{1,0:T(8,128)(2,1)}, bf16[512,512]{1,0:T(8,128)(2,1)}, bf16[512,512]{1,0:T(8,128)(2,1)}, bf16[512,512]{1,0:T(8,128)(2,1)}) custom-call(s32[2,4]{1,0:T(2,128)} %offs.1, bf16[512,512]{1,0:T(8,128)(2,1)} %qh.1, bf16[512,512]{1,0:T(8,128)(2,1)} %kh.1, bf16[512,512]{1,0:T(8,128)(2,1)} %vh.1, bf16[512,2048]{1,0:T(8,128)(2,1)} %wh.1, ...), custom_call_target="tpu_custom_call" | custom-call | flops 4400000000 | bytes 8388608 | tf_op jit(solution)/shard_map/dilated/pallas_call | solution.py:541
  58.3 2.4 %hand_on.1 = (bf16[512,512]{1,0:T(8,128)(2,1)}, bf16[512,512]{1,0:T(8,128)(2,1)}, bf16[512,512]{1,0:T(8,128)(2,1)}, bf16[512,512]{1,0:T(8,128)(2,1)}) custom-call(bf16[512,512]{1,0:T(8,128)(2,1)} %get-tuple-element.8.a, bf16[512,512]{1,0:T(8,128)(2,1)} %get-tuple-element.9.b, bf16[512,512]{1,0:T(8,128)(2,1)} %get-tuple-element.10.c, ...), custom_call_target="tpu_custom_call" | custom-call | tf_op jit(solution)/shard_map/hand_on/pallas_call | solution.py:573

commit v5 on v4

--- a/solution.py
+++ b/solution.py
@@ -48,7 +48,7 @@
            st_l, st_n, q_n, a_n, a_f, f16, att, c_l, c_n, inn, dqt, dqa, dka, dva,
            p1s, p1r, fkv, fo, p5s, p5r, fgr, rz, p8s, p8r,
            ng, nrb, mcs, mcr, mkeep, mxs, mxr,
-           back_n, back_f, ins, outs, ss, rs):
+           back_n, back_f, att_t, ins, outs, ss, rs):
     s = lax.axis_index("seq")
     m = lax.axis_index("mp")
     y, z, xh = s // 16, (s // 2) % NZ, s % 2
@@ -274,6 +274,7 @@
         inv = 1.0 / total
         out = low((o_l[h] * wl + on * wn + of * wf) * inv)
         att[hc(h), :] = out
+        att_t[:, hc(h)] = out.T
         c_l[h, 0:1, :] = wl * inv
         c_l[h, 1:2, :] = wn * inv
         c_l[h, 2:3, :] = wf * inv
@@ -291,7 +292,7 @@
         combine(h)
     def mixed_part(ll, cc, n):
         cols = pl.ds(pl.multiple_of((ll * 2 + cc) * ROWS, ROWS), ROWS)
-        return tn(att[:, 256 * n:256 * n + 256], w[:, cols])
+        return nn(att_t[256 * n:256 * n + 256, :], w[:, cols])
 
     def half(n):
         return pl.ds(256 * n, 256)
@@ -308,13 +309,6 @@
     for n in range(2):
         mcs[0, half(n), :] = low(mixed_part(1 - l, 1 - c, n))
         cm0[n].start()
-    for n in range(2):
-        part = mixed_part(1 - l, c, n)
-        cm0[n].wait()
-        mxs[half(n), :] = low(part + mcr[0, half(n), :].astype(F32))
-        send_mixed(2 * n)
-        send_mixed(2 * n + 1)
-
     for n in range(2):
         for i in (2 * n, 2 * n + 1):
             cg_x[i].wait_recv()
@@ -333,6 +327,13 @@
     for cp in p5:
         cp.start()
     p5r[y] = p5s[y]
+
+    for n in range(2):
+        part = mixed_part(1 - l, c, n)
+        cm0[n].wait()
+        mxs[half(n), :] = low(part + mcr[0, half(n), :].astype(F32))
+        send_mixed(2 * n)
+        send_mixed(2 * n + 1)
 
     def near_bwd(h):
         dd = low(nn(a_n[h], do_[:, hc(h)]))
@@ -520,9 +521,11 @@
 
 
 def hand_on(a, b, c, d, a2, b2, c2, d2, hold, in_sem, out_sem):
-    pairs = [(a, a2), (b, b2), (c, c2), (d, d2)]
-    ins = [pltpu.make_async_copy(x, hold.at[j], in_sem.at[j]) for j, (x, _) in enumerate(pairs)]
-    outs = [pltpu.make_async_copy(hold.at[j], x, out_sem.at[j]) for j, (_, x) in enumerate(pairs)]
+    pairs = [(x, x2, j, pl.ds(256 * n, 256)) for j, (x, x2) in enumerate([(a, a2), (b, b2), (c, c2), (d, d2)])
+             for n in range(2)]
+    ins = [pltpu.make_async_copy(x.at[r], hold.at[j, r], in_sem.at[i]) for i, (x, _, j, r) in enumerate(pairs)]
+    outs = [pltpu.make_async_copy(hold.at[j, r], x, out_sem.at[i])
+            for i, (x, j, r) in enumerate([(x2.at[r], j, r) for _, x2, j, r in pairs])]
     for cp in ins:
         cp.start()
     for i, o in zip(ins, outs):
@@ -562,7 +565,7 @@
             V((4, HEADS, 256, HD), BF), V((3, HEADS, 256, HD), BF),
             V((2, ROWS, ROWS), BF), V((2, ROWS, ROWS), BF), V(wide, F32),
             V(wide, BF), V(wide, BF),
-            V((HEADS, ROWS, HD), BF), V((HEADS, ROWS, 16), BF),
+            V((HEADS, ROWS, HD), BF), V((HEADS, ROWS, 16), BF), V(wide, BF),
             dma((5,)), dma((13,)), dma((84,)), dma((84,)),
         ],
         compiler_params=pltpu.CompilerParams(
@@ -575,7 +578,7 @@
         out_shape=(shape,) * 4,
         in_specs=[hbm] * 4,
         out_specs=(hbm,) * 4,
-        scratch_shapes=[V((4, ROWS, ROWS), BF), dma((4,)), dma((4,))],
+        scratch_shapes=[V((4, ROWS, ROWS), BF), dma((8,)), dma((8,))],
         name="hand_on",
     )(*outs)
 

time: 61 us -> 60.6 us (level)
  no operation moved by 1% of the time
where the time goes in v5:
time: 60.6 us; the launch traced here: 60.3 us
  Pallas kernels  59.5 us (98%)
  between operations  0.8 us (1%)
    pallas_call x1, Pallas kernels, local(): pl.pallas_call(kernel, out_shape=(shape,) * 4, in_specs=[pl.BlockSpec(mem...  57.1 us
    pallas_call x1, Pallas kernels, local(): pl.pallas_call(hand_on, out_shape=(shape,) * 4, in_specs=[hbm] * 4, out_s...  2.4 us

profile of v5, /device:TPU:1, one launch (start us, length us, event | category | flops | bytes accessed | tf_op | source)
XLA Modules:
  0.0 60.3 jit_solution(11842312317003403616)
XLA Ops:
  0.6 57.1 %dilated.1 = (bf16[512,512]{1,0:T(8,128)(2,1)}, bf16[512,512]{1,0:T(8,128)(2,1)}, bf16[512,512]{1,0:T(8,128)(2,1)}, bf16[512,512]{1,0:T(8,128)(2,1)}) custom-call(s32[2,4]{1,0:T(2,128)} %offs.1, bf16[512,512]{1,0:T(8,128)(2,1)} %qh.1, bf16[512,512]{1,0:T(8,128)(2,1)} %kh.1, bf16[512,512]{1,0:T(8,128)(2,1)} %vh.1, bf16[512,2048]{1,0:T(8,128)(2,1)} %wh.1, ...), custom_call_target="tpu_custom_call" | custom-call | flops 4400000000 | bytes 8388608 | tf_op jit(solution)/shard_map/dilated/pallas_call | solution.py:544
  57.7 2.4 %hand_on.1 = (bf16[512,512]{1,0:T(8,128)(2,1)}, bf16[512,512]{1,0:T(8,128)(2,1)}, bf16[512,512]{1,0:T(8,128)(2,1)}, bf16[512,512]{1,0:T(8,128)(2,1)}) custom-call(bf16[512,512]{1,0:T(8,128)(2,1)} %get-tuple-element.8.a, bf16[512,512]{1,0:T(8,128)(2,1)} %get-tuple-element.9.b, bf16[512,512]{1,0:T(8,128)(2,1)} %get-tuple-element.10.c, ...), custom_call_target="tpu_custom_call" | custom-call | tf_op jit(solution)/shard_map/hand_on/pallas_call | solution.py:576
